TPU v7x, 32 devices: a whole 2x2x4 slice. The times are simulated.
32 devices in a mesh: dp: 2 (over core), fsdp: 16 (over z, y, x).
Axes of the slice: x: 2, y: 2, z: 4, core: 2. Of those that a mesh axis runs over, the one named last changes fastest.
Arguments:
- tokens: bfloat16 [512, 196, 768], P(('dp', 'fsdp')), may hold values from -40 to 40
- cotangent: bfloat16 [512, 196, 768], P(('dp', 'fsdp')), may hold values from -6 to 6
- counts: int32 [32, 2], P(('dp', 'fsdp')), may hold values from 1 to 8, as said below
- ln1_gain: bfloat16 [768], P('fsdp'), may hold values from 0.25 to 1.75
- ln1_bias: bfloat16 [768], P('fsdp'), may hold values from -4 to 4
- tok_in: bfloat16 [384, 196], P('fsdp'), may hold values from -0.4375 to 0.4375
- tok_in_bias: bfloat16 [384], P('fsdp'), may hold values from -6 to 6
- tok_out: bfloat16 [384, 196], P('fsdp'), may hold values from -0.4375 to 0.4375
- tok_out_bias: bfloat16 [196], replicated, may hold values from -4 to 4
- ln2_gain: bfloat16 [768], P('fsdp'), may hold values from 0.25 to 1.75
- ln2_bias: bfloat16 [768], P('fsdp'), may hold values from -4 to 4
- ch_in: bfloat16 [768, 3072], P('fsdp'), may hold values from -0.21875 to 0.21875
- ch_in_bias: bfloat16 [3072], P('fsdp'), may hold values from -6 to 6
- ch_out: bfloat16 [3072, 768], P('fsdp'), may hold values from -0.15625 to 0.15625
- ch_out_bias: bfloat16 [768], P('fsdp'), may hold values from -4 to 4
Outputs:
- block_out: bfloat16 [512, 196, 768], P(('dp', 'fsdp'))
- input_grad: bfloat16 [512, 196, 768], P(('dp', 'fsdp'))
- ln1_gain_grad: float32 [768], P('fsdp')
- ln1_bias_grad: float32 [768], P('fsdp')
- tok_in_grad: float32 [384, 196], P('fsdp')
- tok_in_bias_grad: float32 [384], P('fsdp')
- tok_out_grad: float32 [384, 196], P('fsdp')
- tok_out_bias_grad: float32 [196], replicated
- ln2_gain_grad: float32 [768], P('fsdp')
- ln2_bias_grad: float32 [768], P('fsdp')
- ch_in_grad: float32 [768, 3072], P('fsdp')
- ch_in_bias_grad: float32 [3072], P('fsdp')
- ch_out_grad: float32 [3072, 768], P('fsdp')
- ch_out_bias_grad: float32 [768], P('fsdp')
Inputs may be any that keep to these rules, and one draw needn't show every extreme that they name: counts[r, m] is the number of live image slots, the first ones, among the 8 slots of device r in micro-batch m; the value 8 occurs in every draw.
All inputs are finite; a program needn't handle non-finite values.
Results may differ from a plain program's by a relative error of at most 0.0065.
Values may be sent and summed in bfloat16 or wider, within the bound.
A program may use at most 256 MiB of HBM per device.

v0:
```python
import jax
import jax.numpy as jnp
from jax import lax
from jax.sharding import PartitionSpec as P

EPSILON = 1e-06


def normalize(rows_in, gain, shift):
    centre = jnp.mean(rows_in, axis=-1, keepdims=True)
    centred = rows_in - centre
    spread = jnp.mean(centred * centred, axis=-1, keepdims=True)
    return centred * lax.rsqrt(spread + EPSILON) * gain + shift


def smooth(values):
    return jax.nn.gelu(values, approximate=True)


def forward(input_block, token_full, channel_full, output_shift):
    gain_one, shift_one, mixing_input_weight, mixing_input_bias, mixing_output_weight = token_full
    gain_two, shift_two, w_up, bias_up, w_down, bias_down = channel_full
    normalized_rows = normalize(
        input_block, gain_one.astype(jnp.float32), shift_one.astype(jnp.float32)
    )
    normalized_reduced = normalized_rows.astype(jnp.bfloat16)
    preactivation = (
        jnp.einsum(
            "qx,exj->eqj",
            mixing_input_weight,
            normalized_reduced,
            preferred_element_type=jnp.float32,
        )
        + mixing_input_bias.astype(jnp.float32)[None, :, None]
    )
    activation_reduced = smooth(preactivation).astype(jnp.bfloat16)
    branch_output = jnp.einsum(
        "hp,zhi->zpi", mixing_output_weight, activation_reduced, preferred_element_type=jnp.float32
    )
    mixing_rows = input_block + branch_output + output_shift.astype(jnp.float32)[None, :, None]
    normed_two = normalize(mixing_rows, gain_two.astype(jnp.float32), shift_two.astype(jnp.float32))
    normed_two_low = normed_two.astype(jnp.bfloat16)
    pre_two = jnp.einsum(
        "bsd,df->bsf", normed_two_low, w_up, preferred_element_type=jnp.float32
    ) + bias_up.astype(jnp.float32)
    act_two_low = smooth(pre_two).astype(jnp.bfloat16)
    result = (
        mixing_rows
        + jnp.einsum("bsf,fd->bsd", act_two_low, w_down, preferred_element_type=jnp.float32)
        + bias_down.astype(jnp.float32)
    )
    kept = (
        normalized_reduced,
        preactivation,
        activation_reduced,
        mixing_rows,
        normed_two_low,
        pre_two,
        act_two_low,
    )
    return (result, kept)


def backward(grad_out, input_block, kept, token_full, channel_full):
    (
        normalized_reduced,
        preactivation,
        activation_reduced,
        mixing_rows,
        normed_two_low,
        pre_two,
        act_two_low,
    ) = kept
    gain_one, shift_one, mixing_input_weight, mixing_input_bias, mixing_output_weight = token_full
    gain_two, shift_two, w_up, bias_up, w_down, bias_down = channel_full
    grad_out_low = grad_out.astype(jnp.bfloat16)
    grad_act_two = jnp.einsum(
        "bsd,fd->bsf", grad_out_low, w_down, preferred_element_type=jnp.float32
    )
    grad_w_down = jnp.einsum(
        "bsf,bsd->fd", act_two_low, grad_out_low, preferred_element_type=jnp.float32
    )
    grad_bias_down = jnp.sum(grad_out, axis=(0, 1))
    grad_pre_two = jax.vjp(smooth, pre_two)[1](grad_act_two)[0]
    grad_bias_up = jnp.sum(grad_pre_two, axis=(0, 1))
    grad_pre_two_low = grad_pre_two.astype(jnp.bfloat16)
    grad_normed_two = jnp.einsum(
        "bsf,df->bsd", grad_pre_two_low, w_up, preferred_element_type=jnp.float32
    )
    grad_w_up = jnp.einsum(
        "bsd,bsf->df", normed_two_low, grad_pre_two_low, preferred_element_type=jnp.float32
    )
    norm_two_back = jax.vjp(
        normalize, mixing_rows, gain_two.astype(jnp.float32), shift_two.astype(jnp.float32)
    )[1]
    grad_through, grad_gain_two, grad_shift_two = norm_two_back(grad_normed_two)
    grad_mixed = grad_out + grad_through
    grad_out_shift = jnp.sum(grad_mixed, axis=(0, 2))
    mixing_gradient_reduced = grad_mixed.astype(jnp.bfloat16)
    grad_act = jnp.einsum(
        "qx,exj->eqj",
        mixing_output_weight,
        mixing_gradient_reduced,
        preferred_element_type=jnp.float32,
    )
    grad_w_mix_out = jnp.einsum(
        "oaq,oeq->ae",
        activation_reduced,
        mixing_gradient_reduced,
        preferred_element_type=jnp.float32,
    )
    grad_pre = jax.vjp(smooth, preactivation)[1](grad_act)[0]
    grad_bias_mix_in = jnp.sum(grad_pre, axis=(0, 2))
    preactivation_gradient_reduced = grad_pre.astype(jnp.bfloat16)
    grad_normed = jnp.einsum(
        "hp,zhi->zpi",
        mixing_input_weight,
        preactivation_gradient_reduced,
        preferred_element_type=jnp.float32,
    )
    grad_w_mix_in = jnp.einsum(
        "oaq,oeq->ae",
        preactivation_gradient_reduced,
        normalized_reduced,
        preferred_element_type=jnp.float32,
    )
    norm_one_back = jax.vjp(
        normalize, input_block, gain_one.astype(jnp.float32), shift_one.astype(jnp.float32)
    )[1]
    grad_inner, grad_gain_one, grad_shift_one = norm_one_back(grad_normed)
    grad_x = grad_mixed + grad_inner
    grad_list = (
        grad_gain_one,
        grad_shift_one,
        grad_w_mix_in,
        grad_bias_mix_in,
        grad_w_mix_out,
        grad_gain_two,
        grad_shift_two,
        grad_w_up,
        grad_bias_up,
        grad_w_down,
        grad_bias_down,
    )
    return (grad_x, grad_list, grad_out_shift)


def per_device(
    tokens,
    cotangent,
    counts,
    ln1_gain,
    ln1_bias,
    tok_in,
    tok_in_bias,
    tok_out,
    tok_out_bias,
    ln2_gain,
    ln2_bias,
    ch_in,
    ch_in_bias,
    ch_out,
    ch_out_bias,
):
    micro_total = counts.shape[1]
    per_micro = tokens.shape[0] // micro_total
    outputs = []
    input_grads = []
    grad_sums = None
    shift_sum = jnp.zeros((tok_out_bias.shape[0],), jnp.float32)
    for micro in range(micro_total):
        lower = micro * per_micro
        input_block = tokens[lower : lower + per_micro].astype(jnp.float32)
        live_rows = (jnp.arange(per_micro) < counts[0, micro]).astype(jnp.float32)[:, None, None]
        grad_out = cotangent[lower : lower + per_micro].astype(jnp.float32) * live_rows
        token_full = (
            lax.all_gather(ln1_gain, "fsdp", axis=0, tiled=True),
            lax.all_gather(ln1_bias, "fsdp", axis=0, tiled=True),
            lax.all_gather(tok_in, "fsdp", axis=0, tiled=True),
            lax.all_gather(tok_in_bias, "fsdp", axis=0, tiled=True),
            lax.all_gather(tok_out, "fsdp", axis=0, tiled=True),
        )
        channel_full = (
            lax.all_gather(ln2_gain, "fsdp", axis=0, tiled=True),
            lax.all_gather(ln2_bias, "fsdp", axis=0, tiled=True),
            lax.all_gather(ch_in, "fsdp", axis=0, tiled=True),
            lax.all_gather(ch_in_bias, "fsdp", axis=0, tiled=True),
            lax.all_gather(ch_out, "fsdp", axis=0, tiled=True),
            lax.all_gather(ch_out_bias, "fsdp", axis=0, tiled=True),
        )
        result, kept = forward(input_block, token_full, channel_full, tok_out_bias)
        outputs.append((result * live_rows).astype(jnp.bfloat16))
        token_back = (
            lax.all_gather(ln1_gain, "fsdp", axis=0, tiled=True),
            lax.all_gather(ln1_bias, "fsdp", axis=0, tiled=True),
            lax.all_gather(tok_in, "fsdp", axis=0, tiled=True),
            lax.all_gather(tok_in_bias, "fsdp", axis=0, tiled=True),
            lax.all_gather(tok_out, "fsdp", axis=0, tiled=True),
        )
        channel_back = (
            lax.all_gather(ln2_gain, "fsdp", axis=0, tiled=True),
            lax.all_gather(ln2_bias, "fsdp", axis=0, tiled=True),
            lax.all_gather(ch_in, "fsdp", axis=0, tiled=True),
            lax.all_gather(ch_in_bias, "fsdp", axis=0, tiled=True),
            lax.all_gather(ch_out, "fsdp", axis=0, tiled=True),
            lax.all_gather(ch_out_bias, "fsdp", axis=0, tiled=True),
        )
        grad_x, grad_list, grad_out_shift = backward(
            grad_out, input_block, kept, token_back, channel_back
        )
        input_grads.append(grad_x.astype(jnp.bfloat16))
        shift_sum = shift_sum + grad_out_shift
        grad_sums = (
            grad_list
            if grad_sums is None
            else tuple(jax.tree.map(jnp.add, tuple(grad_sums), tuple(grad_list)))
        )
    grad_sums = (
        lax.psum_scatter(grad_sums[0], "fsdp", scatter_dimension=0, tiled=True),
        lax.psum_scatter(grad_sums[1], "fsdp", scatter_dimension=0, tiled=True),
        lax.psum_scatter(grad_sums[2], "fsdp", scatter_dimension=0, tiled=True),
        lax.psum_scatter(grad_sums[3], "fsdp", scatter_dimension=0, tiled=True),
        lax.psum_scatter(grad_sums[4], "fsdp", scatter_dimension=0, tiled=True),
        lax.psum_scatter(grad_sums[5], "fsdp", scatter_dimension=0, tiled=True),
        lax.psum_scatter(grad_sums[6], "fsdp", scatter_dimension=0, tiled=True),
        lax.psum_scatter(grad_sums[7], "fsdp", scatter_dimension=0, tiled=True),
        lax.psum_scatter(grad_sums[8], "fsdp", scatter_dimension=0, tiled=True),
        lax.psum_scatter(grad_sums[9], "fsdp", scatter_dimension=0, tiled=True),
        lax.psum_scatter(grad_sums[10], "fsdp", scatter_dimension=0, tiled=True),
    )
    shards = lax.psum(
        (
            grad_sums[0],
            grad_sums[1],
            grad_sums[2],
            grad_sums[3],
            grad_sums[4],
            grad_sums[5],
            grad_sums[6],
            grad_sums[7],
            grad_sums[8],
            grad_sums[9],
            grad_sums[10],
        ),
        "dp",
    )
    shift_total = lax.psum(shift_sum, ("dp", "fsdp"))
    block_out = jnp.concatenate(outputs, axis=0)
    input_grad = jnp.concatenate(input_grads, axis=0)
    return (
        block_out,
        input_grad,
        shards[0],
        shards[1],
        shards[2],
        shards[3],
        shards[4],
        shift_total,
        shards[5],
        shards[6],
        shards[7],
        shards[8],
        shards[9],
        shards[10],
    )


def solution(mesh):
    return jax.shard_map(
        per_device,
        mesh=mesh,
        in_specs=(
            P(("dp", "fsdp"), None, None),
            P(("dp", "fsdp"), None, None),
            P(("dp", "fsdp"), None),
            P("fsdp"),
            P("fsdp"),
            P("fsdp", None),
            P("fsdp"),
            P("fsdp", None),
            P(),
            P("fsdp"),
            P("fsdp"),
            P("fsdp", None),
            P("fsdp"),
            P("fsdp", None),
            P("fsdp"),
        ),
        out_specs=(
            P(("dp", "fsdp"), None, None),
            P(("dp", "fsdp"), None, None),
            P("fsdp"),
            P("fsdp"),
            P("fsdp", None),
            P("fsdp"),
            P("fsdp", None),
            P(),
            P("fsdp"),
            P("fsdp"),
            P("fsdp", None),
            P("fsdp"),
            P("fsdp", None),
            P("fsdp"),
        ),
        check_vma=False,
    )
```

profile of v0, /device:TPU:0, one launch (start us, length us, event | category | flops | bytes accessed | tf_op | source)
XLA Modules:
  0.0 945.7 jit_solution(6940903318540957191)
XLA Ops:
  17.9 79.6 %all-reduce.17 = (bf16[768]{0:T(1024)(128)(2,1)S(1)}, bf16[768]{0:T(1024)(128)(2,1)S(1)}, bf16[384]{0:T(512)(128)(2,1)S(1)}, bf16[768]{0:T(1024)(128)(2,1)}, bf1...) all-reduce(bf16[768]{0:T(1024)(128)(2,1)S(1)} %dynamic-update-slice, ...), channel_id=1, replica_groups=mesh['dp'=2,'fsdp'=16] {'fsdp'}, use_global_device_ids=true, to_apply=%add.1 | all-reduce | flops 7296 | bytes 29184
  101.1 37.1 %all_gather.24 = bf16[384,196]{1,0:T(8,128)(2,1)S(1)} all-gather(bf16[24,196]{1,0:T(8,128)(2,1)S(1)} %copy-done.41), channel_id=1, replica_groups=mesh['dp'=2,'fsdp'=16] {'fsdp'}, dimensions={0}, use_global_device_ids=true | all-gather | bytes 159936 | tf_op jit(solution)/shard_map/all_gather | solution.py:179
  138.3 39.9 %all_gather.26 = bf16[384,196]{1,0:T(8,128)(2,1)S(1)} all-gather(bf16[24,196]{1,0:T(8,128)(2,1)S(1)} %copy-done.42), channel_id=1, replica_groups=mesh['dp'=2,'fsdp'=16] {'fsdp'}, dimensions={0}, use_global_device_ids=true | all-gather | bytes 159936 | tf_op jit(solution)/shard_map/all_gather | solution.py:181
  186.8 4.9 fusion.165
  197.0 4.9 fusion.164
  206.5 15.3 %fusion.77 = f32[8,196,3072]{2,1,0:T(8,128)} fusion(bf16[768,3072]{1,0:T(8,128)(2,1)} %all-gather.3.cloned.1.call-done, f32[8,196,768]{2,1,0:T(8,128)} %copy-done.6, f32[768]{0:T(1024)S(1)} %convert_element_type.130, f32[768]{0:T(1024)S(1)} %convert_element_type.129, f32[8,196]{1,0:T(8,128)S(1)} %fusion.149, f32[8,196]{1,0:T(8,128)S(1)} %broadcast_multiply_fusion.2), kind=kOutput, calls=%fused_computation.125 | convolution fusion | flops 7404773376 | bytes 28821760 | tf_op jit(solution)/shard_map/bsd,df->bsf/dot_general | solution.py:43
  221.8 23.8 %fusion.168 = (f32[3072]{0:T(1024)}, bf16[8,196,3072]{2,1,0:T(8,128)(2,1)S(1)}) fusion(f32[8,196,3072]{2,1,0:T(8,128)} %fusion.77, f32[3072]{0:T(1024)S(1)} %convert_element_type.132, bf16[3072,768]{1,0:T(8,128)(2,1)} %all-gather.5.cloned.1.call-done, f32[8]{0:T(128)S(1)} %get-tuple-element.122, bf16[8,196,768]{2,0,1:T(8,128)(2,1)S(1)} %get-tuple-element.84), kind=kOutput, calls=%fused_computation.200 | convolution fusion | flops 7508333568 | bytes 36053024 | tf_op jit(solution)/shard_map/bsd,fd->bsf/dot_general | solution.py:77
  249.3 12.2 %fusion.61 = f32[768,3072,1]{1,0,2:T(8,128)} fusion(bf16[8,196,3072]{2,1,0:T(8,128)(2,1)S(1)} %get-tuple-element.116, f32[8,196,768]{2,1,0:T(8,128)S(1)} %bitcast.181, f32[768]{0:T(1024)S(1)} %convert_element_type.130, f32[768]{0:T(1024)S(1)} %convert_element_type.129, f32[8,196]{1,0:T(8,128)S(1)} %fusion.149, f32[8,196]{1,0:T(8,128)S(1)} %broadcast_multiply_fusion.2), kind=kOutput, calls=%fused_computation.102 | convolution fusion | flops 7404773376 | bytes 23906560 | tf_op jit(solution)/shard_map/bsd,bsf->df/dot_general | solution.py:90
  261.5 15.0 %fusion.75 = f32[8,196,3072]{2,1,0:T(8,128)} fusion(bf16[768,3072]{1,0:T(8,128)(2,1)S(1)} %copy-done.49, f32[8,196,768]{2,1,0:T(8,128)} %copy-done.7, f32[8,196]{1,0:T(8,128)S(1)} %fusion.151, f32[8,196]{1,0:T(8,128)S(1)} %broadcast_multiply_fusion, f32[768]{0:T(1024)S(1)} %convert_element_type.130, f32[768]{0:T(1024)S(1)} %convert_element_type.129), kind=kOutput, calls=%fused_computation.123 | convolution fusion | flops 7404773376 | bytes 28821760 | tf_op jit(solution)/shard_map/bsd,df->bsf/dot_general | solution.py:43
  276.5 24.8 %fusion.169 = (f32[3072]{0:T(1024)}, bf16[8,196,3072]{2,1,0:T(8,128)(2,1)}) fusion(f32[8,196,3072]{2,1,0:T(8,128)} %fusion.75, f32[3072]{0:T(1024)S(1)} %convert_element_type.132, bf16[3072,768]{1,0:T(8,128)(2,1)} %all-gather.5.cloned.1.call-done, f32[8]{0:T(128)S(1)} %get-tuple-element.121, bf16[8,196,768]{2,0,1:T(8,128)(2,1)S(1)} %copy-done.11), kind=kOutput, calls=%fused_computation.201 | convolution fusion | flops 7508333568 | bytes 36053024 | tf_op jit(solution)/shard_map/bsd,fd->bsf/dot_general | solution.py:77
  301.3 16.3 %bitcast_add_fusion.1 = f32[768,3072]{1,0:T(8,128)} fusion(f32[768,3072,1]{1,0,2:T(8,128)} %fusion.61, bf16[8,196,3072]{2,1,0:T(8,128)(2,1)} %get-tuple-element.118, f32[8,196,768]{2,1,0:T(8,128)S(1)} %bitcast.185, f32[8,196]{1,0:T(8,128)S(1)} %fusion.151, f32[8,196]{1,0:T(8,128)S(1)} %broadcast_multiply_fusion, f32[768]{0:T(1024)S(1)} %convert_element_type.130, ...), kind=kOutput, calls=%fused_computation.35 | convolution fusion | flops 7407132672 | bytes 33343744 | tf_op jit(solution)/shard_map/bsd,bsf->df/dot_general | solution.py:90
  317.8 19.7 %fusion.129 = f32[3072,768,1]{1,0,2:T(8,128)} fusion(f32[8]{0:T(128)S(1)} %get-tuple-element.122, bf16[8,196,768]{2,0,1:T(8,128)(2,1)S(1)} %get-tuple-element.84, f32[8,196,3072]{2,1,0:T(8,128)} %fusion.77, f32[3072]{0:T(1024)S(1)} %convert_element_type.132), kind=kOutput, calls=%fused_computation.151 | convolution fusion | flops 7450533888 | bytes 31125536 | tf_op jit(solution)/shard_map/bsf,bsd->fd/dot_general | solution.py:80
  337.4 20.9 %bitcast_add_fusion = f32[3072,768]{1,0:T(8,128)} fusion(f32[3072,768,1]{1,0,2:T(8,128)} %fusion.129, f32[8]{0:T(128)S(1)} %get-tuple-element.121, bf16[8,196,768]{2,0,1:T(8,128)(2,1)S(1)} %copy-done.12, f32[8,196,3072]{2,1,0:T(8,128)} %fusion.75, f32[3072]{0:T(1024)S(1)} %convert_element_type.132), kind=kOutput, calls=%fused_computation.34 | convolution fusion | flops 7452893184 | bytes 40562720 | tf_op jit(solution)/shard_map/bsf,bsd->fd/dot_general | solution.py:80
  360.5 14.3 %fusion.57 = f32[8,196,768]{2,1,0:T(8,128)} fusion(bf16[8,196,3072]{2,1,0:T(8,128)(2,1)} %get-tuple-element.118, bf16[768,3072]{1,0:T(8,128)(2,1)} %all-gather.3.cloned.1.call-done), kind=kOutput, calls=%fused_computation.94 | convolution fusion | flops 7398752256 | bytes 19169280 | tf_op jit(solution)/shard_map/bsf,df->bsd/dot_general | solution.py:87
  374.8 17.9 %fusion.157 = (f32[768]{0:T(1024)S(1)}, f32[8,196]{1,0:T(8,128)S(1)}, f32[8,196]{1,0:T(8,128)S(1)}, f32[768]{0:T(1024)S(1)}, f32[8,196,768]{2,1,0:T(8,128)}) fusion(f32[768]{0:T(1024)S(1)} %convert_element_type.129, f32[8,196,768]{2,1,0:T(8,128)S(1)} %bitcast.183, f32[8,196]{1,0:T(8,128)S(1)} %broadcast_multiply_fusion.2, f32[8,196,768]{2,1,0:T(8,128)} %fusion.57, ...), kind=kOutput, calls=%fused_computation.189 | convolution fusion | flops 7410789376 | bytes 33654272 | tf_op jit(solution)/shard_map/bsf,df->bsd/dot_general | solution.py:87
  392.8 7.7 multiply_reduce_fusion.1
  400.5 14.5 %fusion.159 = (f32[196]{0:T(256)S(1)}, f32[8,196,768]{2,1,0:T(8,128)}, f32[768]{0:T(1024)S(1)}, f32[768]{0:T(1024)S(1)}, f32[196]{0:T(256)S(1)}, /*index=5*/f32[8,196,768]{2,1,0:T(8,128)}) fusion(f32[8,196]{1,0:T(8,128)S(1)} %negate_multiply_fusion.3, f32[8,196]{1,0:T(8,128)S(1)} %multiply_multiply_fusion.11, f32[8,196,768]{2,1,0:T(8,128)S(1)} %bitcast.183, ...), kind=kLoop, calls=%fused_computation.191 | loop fusion | flops 28899448 | bytes 33779296 | tf_op jit(solution)/shard_map/reduce_sum | solution.py:98
  415.1 13.7 %fusion.166 = (f32[384]{0:T(512)S(1)}, bf16[8,384,768]{1,2,0:T(8,128)(2,1)}) fusion(f32[8,768,384]{2,1,0:T(8,128)} %copy-done.8, f32[384]{0:T(512)S(1)} %copy-done.47, bf16[384,196]{1,0:T(8,128)(2,1)S(1)} %copy-done.26, f32[8,196,768]{2,1,0:T(8,128)} %get-tuple-element.83), kind=kOutput, calls=%fused_computation.198 | convolution fusion | flops 977952384 | bytes 19126272 | tf_op jit(solution)/shard_map/qx,exj->eqj/dot_general | solution.py:100
  433.7 9.4 fusion.167
  443.2 8.2 fusion.49
  451.5 4.9 fusion.111
  456.4 6.8 fusion.105
  467.8 6.2 fusion.124
  474.0 20.1 %multiply_convert_fusion.3 = bf16[8,196,768]{2,1,0:T(8,128)(2,1)} fusion(f32[8,196,768]{2,1,0:T(8,128)} %copy-done.6, f32[8]{0:T(128)S(1)} %get-tuple-element.122, f32[768]{0:T(1024)S(1)} %convert_element_type.134, bf16[3072,768]{1,0:T(8,128)(2,1)} %all-gather.5.cloned.1.call-done, f32[8,196,3072]{2,1,0:T(8,128)} %fusion.77, ...), kind=kOutput, calls=%fused_computation.112 | convolution fusion | flops 7451738112 | bytes 31226912 | tf_op jit(solution)/shard_map/bsf,fd->bsd/dot_general | solution.py:49
  494.2 19.9 %multiply_convert_fusion.2 = bf16[8,196,768]{2,1,0:T(8,128)(2,1)} fusion(f32[8,196,768]{2,1,0:T(8,128)} %copy-done.7, f32[8]{0:T(128)S(1)} %get-tuple-element.121, f32[768]{0:T(1024)S(1)} %convert_element_type.134, bf16[3072,768]{1,0:T(8,128)(2,1)} %all-gather.5.cloned.1.call-done, f32[8,196,3072]{2,1,0:T(8,128)} %fusion.75, ...), kind=kOutput, calls=%fused_computation.109 | convolution fusion | flops 7451738112 | bytes 31226912 | tf_op jit(solution)/shard_map/bsf,fd->bsd/dot_general | solution.py:49
  523.0 73.0 %all-reduce.14 = (f32[768]{0:T(1024)S(1)}, f32[768]{0:T(1024)S(1)}, f32[384]{0:T(512)S(1)}, f32[768]{0:T(1024)S(1)}, f32[768]{0:T(1024)S(1)}, /*index=5*/f32[3072]{0:T(1024)S(1)}, f32[768]{0:T(1024)S(1)}) all-reduce(f32[768]{0:T(1024)S(1)} %add.316, f32[768]{0:T(1024)S(1)} %add.317, ...), channel_id=2, replica_groups=mesh['dp'=2,'fsdp'=16] {'fsdp'}, use_global_device_ids=true, to_apply=%region_18.0.clone | all-reduce | flops 7296 | bytes 58368
  596.4 65.4 %reduce-scatter.11.cloned.1.call-done = f32[192,768]{1,0:T(8,128)} async-done(((f32[3072,768]{1,0:T(8,128)}), f32[192,768]{1,0:T(8,128)}) %reduce-scatter.11.cloned.1.call-update) | async-done | bytes 589840 | tf_op jit(solution)/shard_map/reduce_scatter | solution.py:228
  661.8 9.3 add_convert_fusion.1
  679.0 39.1 %psum.89 = f32[196]{0:T(256)} all-reduce(f32[196]{0:T(256)S(1)} %add.321), channel_id=1, replica_groups=mesh['dp'=2,'fsdp'=16] {'dp','fsdp'}, use_global_device_ids=true, to_apply=%region_34.0 | all-reduce | flops 196 | bytes 1568 | tf_op jit(solution)/shard_map/psum | solution.py:247
  718.1 69.1 %reduce-scatter.7.cloned.1.call-done = f32[24,196]{1,0:T(8,128)} async-done(((f32[384,196]{1,0:T(8,128)}), f32[24,196]{1,0:T(8,128)}) %reduce-scatter.7.cloned.1.call-update) | async-done | bytes 18832 | tf_op jit(solution)/shard_map/reduce_scatter | solution.py:223
  787.2 126.2 %reduce-scatter.5.cloned.1.call-done = f32[24,196]{1,0:T(8,128)} async-done(((f32[384,196]{1,0:T(8,128)}), f32[24,196]{1,0:T(8,128)}) %reduce-scatter.5.cloned.1.call-update) | async-done | bytes 18832 | tf_op jit(solution)/shard_map/reduce_scatter | solution.py:221
  918.2 16.7 %all-reduce.20.cloned.1.call-done = (f32[48,3072]{1,0:T(8,128)}, f32[192,768]{1,0:T(8,128)}) async-done(((f32[48,3072]{1,0:T(8,128)}, f32[192,768]{1,0:T(8,128)}), (f32[48,3072]{1,0:T(8,128)}, f32[192,768]{1,0:T(8,128)})) %all-reduce.20.cloned.1.call-update) | async-done | bytes 1179664 | tf_op jit(solution)/shard_map/psum | solution.py:231
  (249 shorter events, 69.4 us)
Async XLA Ops:
  7.2 199.3 %all-gather.3.cloned.1.call-start = ((), (), s32[]{:S(2)}) async-start(), calls=%async_computation.4 | async-start | bytes 5013504 | tf_op jit(solution)/shard_map/all_gather | solution.py:186
  7.9 213.9 %all-gather.5.cloned.1.call-start = ((), (), s32[]{:S(2)}) async-start(), calls=%async_computation.5 | async-start | bytes 5013504 | tf_op jit(solution)/shard_map/all_gather | solution.py:188
  8.7 587.8 %reduce-scatter.9.cloned.1.call-start = ((), (), s32[]{:S(2)}) async-start(), calls=%async_computation.8 | async-start | bytes 10027008 | tf_op jit(solution)/shard_map/reduce_scatter | solution.py:226
  97.5 96.0 %copy-start.21 = (f32[768]{0:T(1024)}, f32[768]{0:T(1024)S(1)}, u32[]{:S(2)}) copy-start(f32[768]{0:T(1024)S(1)} %convert_element_type.123) | copy-start | bytes 9220
  97.5 96.0 %copy-start.29 = (f32[768]{0:T(1024)}, f32[768]{0:T(1024)S(1)}, u32[]{:S(2)}) copy-start(f32[768]{0:T(1024)S(1)} %convert_element_type.124) | copy-start | bytes 9220
  97.5 40.7 %copy-start.42 = (bf16[24,196]{1,0:T(8,128)(2,1)S(1)}, bf16[24,196]{1,0:T(8,128)(2,1)}, u32[]{:S(2)}) copy-start(bf16[24,196]{1,0:T(8,128)(2,1)} %param.22) | copy-start | bytes 28228
  97.6 80.6 %copy-start.50 = (bf16[196]{0:T(256)(128)(2,1)S(1)}, bf16[196]{0:T(256)(128)(2,1)}, u32[]{:S(2)}) copy-start(bf16[196]{0:T(256)(128)(2,1)} %param.23) | copy-start | bytes 1180
  97.6 80.6 %copy-start.48 = (s32[1,2]{1,0:T(1,128)S(1)}, s32[1,2]{1,0:T(1,128)}, u32[]{:S(2)}) copy-start(s32[1,2]{1,0:T(1,128)} %param.17) | copy-start | bytes 28
  100.3 86.5 %copy-start = (bf16[8,196,768]{2,0,1:T(8,128)(2,1)}, bf16[8,196,768]{2,0,1:T(8,128)(2,1)S(1)}, u32[]{:S(2)}) copy-start(bf16[8,196,768]{2,0,1:T(8,128)(2,1)S(1)} %get-tuple-element.86) | copy-start | bytes 7225348
  100.3 96.6 %copy-start.2 = (bf16[8,196,768]{2,0,1:T(8,128)(2,1)}, bf16[8,196,768]{2,0,1:T(8,128)(2,1)S(1)}, u32[]{:S(2)}) copy-start(bf16[8,196,768]{2,0,1:T(8,128)(2,1)S(1)} %get-tuple-element.87) | copy-start | bytes 7225348
  138.2 55.3 %copy-start.13 = (bf16[384,196]{1,0:T(8,128)(2,1)}, bf16[384,196]{1,0:T(8,128)(2,1)S(1)}, u32[]{:S(2)}) copy-start(bf16[384,196]{1,0:T(8,128)(2,1)S(1)} %all_gather.24) | copy-start | bytes 451588
  138.2 58.7 %copy-start.46 = (f32[384]{0:T(512)}, f32[384]{0:T(512)S(1)}, u32[]{:S(2)}) copy-start(f32[384]{0:T(512)S(1)} %convert_element_type.126) | copy-start | bytes 4612
  178.1 18.8 %copy-start.25 = (bf16[384,196]{1,0:T(8,128)(2,1)}, bf16[384,196]{1,0:T(8,128)(2,1)S(1)}, u32[]{:S(2)}) copy-start(bf16[384,196]{1,0:T(8,128)(2,1)S(1)} %all_gather.26) | copy-start | bytes 451588
  193.5 52.1 %copy-start.39 = (f32[8,196]{1,0:T(8,128)}, f32[8,196]{1,0:T(8,128)S(1)}, u32[]{:S(2)}) copy-start(f32[8,196]{1,0:T(8,128)S(1)} %fusion.149) | copy-start | bytes 18820
  206.5 42.8 %slice-start.2 = ((s8[4915200]{0:T(1024)(128)(4,1)}), s8[720896]{0:T(1024)(128)(4,1)S(1)}, s32[]{:S(2)}) async-start(s8[4915200]{0:T(1024)(128)(4,1)} %bitcast.180), calls=%async_computation.13 | async-start | bytes 1441792
  221.8 27.5 %slice-start.3 = ((s8[4915200]{0:T(1024)(128)(4,1)}), s8[4194304]{0:T(1024)(128)(4,1)S(1)}, s32[]{:S(2)}) async-start(s8[4915200]{0:T(1024)(128)(4,1)} %bitcast.180), calls=%async_computation.14 | async-start | bytes 8388608
  261.5 39.8 %slice-start.6 = ((s8[4915200]{0:T(1024)(128)(4,1)}), s8[4194304]{0:T(1024)(128)(4,1)S(1)}, s32[]{:S(2)}) async-start(s8[4915200]{0:T(1024)(128)(4,1)} %bitcast.184), calls=%async_computation.17 | async-start | bytes 8388608
  276.5 24.8 %slice-start.7 = ((s8[4915200]{0:T(1024)(128)(4,1)}), s8[720896]{0:T(1024)(128)(4,1)S(1)}, s32[]{:S(2)}) async-start(s8[4915200]{0:T(1024)(128)(4,1)} %bitcast.184), calls=%async_computation.18 | async-start | bytes 1441792
  317.7 344.1 %reduce-scatter.11.cloned.1.call-start = ((), (), s32[]{:S(2)}) async-start(), calls=%async_computation.9 | async-start | bytes 10027008 | tf_op jit(solution)/shard_map/reduce_scatter | solution.py:228
  317.8 19.7 %copy-start.12 = (bf16[8,196,768]{2,0,1:T(8,128)(2,1)S(1)}, bf16[8,196,768]{2,0,1:T(8,128)(2,1)}, u32[]{:S(2)}) copy-start(bf16[8,196,768]{2,0,1:T(8,128)(2,1)} %get-tuple-element.85) | copy-start | bytes 7225348
  358.4 428.9 %reduce-scatter.7.cloned.1.call-start = ((), (), s32[]{:S(2)}) async-start(), calls=%async_computation.7 | async-start | bytes 417792 | tf_op jit(solution)/shard_map/reduce_scatter | solution.py:223
  374.8 17.9 %copy-start.38 = (f32[8,196]{1,0:T(8,128)S(1)}, f32[8,196]{1,0:T(8,128)}, u32[]{:S(2)}) copy-start(f32[8,196]{1,0:T(8,128)} %copy-done.37) | copy-start | bytes 18820
  374.8 17.9 %copy-start.36 = (f32[8,196]{1,0:T(8,128)S(1)}, f32[8,196]{1,0:T(8,128)}, u32[]{:S(2)}) copy-start(f32[8,196]{1,0:T(8,128)} %copy-done.35) | copy-start | bytes 18820
  374.8 18.0 %copy-start.40 = (f32[8,196]{1,0:T(8,128)S(1)}, f32[8,196]{1,0:T(8,128)}, u32[]{:S(2)}) copy-start(f32[8,196]{1,0:T(8,128)} %copy-done.39) | copy-start | bytes 18820
  400.5 33.1 %slice-start.11 = ((s8[9437184]{0:T(1024)(128)(4,1)}), s8[4194304]{0:T(1024)(128)(4,1)S(1)}, s32[]{:S(2)}) async-start(s8[9437184]{0:T(1024)(128)(4,1)} %bitcast.188), calls=%async_computation.22 | async-start | bytes 8388608
  415.1 18.6 %slice-start.12 = ((s8[9437184]{0:T(1024)(128)(4,1)}), s8[4194304]{0:T(1024)(128)(4,1)S(1)}, s32[]{:S(2)}) async-start(s8[9437184]{0:T(1024)(128)(4,1)} %bitcast.188), calls=%async_computation.23 | async-start | bytes 8388608
  415.1 18.6 %slice-start.13 = ((s8[9437184]{0:T(1024)(128)(4,1)}), s8[1048576]{0:T(1024)(128)(4,1)S(1)}, s32[]{:S(2)}) async-start(s8[9437184]{0:T(1024)(128)(4,1)} %bitcast.188), calls=%async_computation.24 | async-start | bytes 2097152
  467.7 445.7 %reduce-scatter.5.cloned.1.call-start = ((), (), s32[]{:S(2)}) async-start(), calls=%async_computation.6 | async-start | bytes 417792 | tf_op jit(solution)/shard_map/reduce_scatter | solution.py:221
  474.0 460.8 %all-reduce.20.cloned.1.call-start = ((), (), s32[]{:S(2)}) async-start(), calls=%async_computation.10 | async-start | bytes 2359296 | tf_op jit(solution)/shard_map/psum | solution.py:231
  474.0 40.0 %slice-start = ((s8[4915200]{0:T(1024)(128)(4,1)}), s8[4194304]{0:T(1024)(128)(4,1)S(1)}, s32[]{:S(2)}) async-start(s8[4915200]{0:T(1024)(128)(4,1)} %bitcast.178), calls=%async_computation.11 | async-start | bytes 8388608
  494.2 19.9 %copy-start.4 = (bf16[8,196,768]{2,0,1:T(8,128)(2,1)S(1)}, bf16[8,196,768]{2,0,1:T(8,128)(2,1)}, u32[]{:S(2)}) copy-start(bf16[8,196,768]{2,0,1:T(8,128)(2,1)} %copy-done.2) | copy-start | bytes 7225348
  494.2 19.9 %slice-start.1 = ((s8[4915200]{0:T(1024)(128)(4,1)}), s8[720896]{0:T(1024)(128)(4,1)S(1)}, s32[]{:S(2)}) async-start(s8[4915200]{0:T(1024)(128)(4,1)} %bitcast.178), calls=%async_computation.12 | async-start | bytes 1441792
  (48 other events, 395.8 us)
Sparse Core Ops, SparseCore 0:
  10.8 85.5 all-gather.2
  99.2 80.9 all-gather.4
  317.8 166.9 reduce-scatter.8
  491.3 170.4 reduce-scatter.10
  666.9 120.2 reduce-scatter.6
  793.0 120.3 reduce-scatter.4
  915.8 18.9 all-reduce.19
where the time goes:
time: 950 us; the launch traced here: 946 us
  matrix products  295 us (31%)
  waiting for transfers between devices  279 us (29%)
  blocking collectives  273 us (29%)
  other arithmetic  48.3 us (5%)
  local copies, waits for them, and re-layouts  30.7 us (3%)
  between operations  19.4 us (2%)
    unnamed x2, blocking collectives  153 us
    reduce_scatter x1, waiting for transfers between devices, per_device(): lax.psum_scatter(grad_sums[2], 'fsdp', scatter_dimension=0, tiled=True)  126 us
    reduce_scatter x1, waiting for transfers between devices, per_device(): lax.psum_scatter(grad_sums[4], 'fsdp', scatter_dimension=0, tiled=True)  69.1 us
    reduce_scatter x1, waiting for transfers between devices, per_device(): lax.psum_scatter(grad_sums[9], 'fsdp', scatter_dimension=0, tiled=True)  65.4 us
    dot_general x2, matrix products, backward(): jnp.einsum('bsd,fd->bsf', grad_out_low, w_down, preferred_element_type=jn...  48.6 us
    dot_general x2, matrix products, backward(): jnp.einsum('bsf,bsd->fd', act_two_low, grad_out_low, preferred_element_ty...  40.6 us
    dot_general x2, matrix products, forward(): jnp.einsum('bsf,fd->bsd', act_two_low, w_down, preferred_element_type=jnp...  40 us
    all_gather x1, blocking collectives, per_device(): lax.all_gather(tok_out, 'fsdp', axis=0, tiled=True)  39.9 us
  transfers between devices with their start and end apart: 7, of which 4 were waited for; matrix products, arithmetic and copies ran while one was open for 29% of the time, Pallas kernels for 0%

commit v1 on v0

--- a/solution.py
+++ b/solution.py
@@ -1,6 +1,8 @@
 import jax
 import jax.numpy as jnp
 from jax import lax
+from jax.experimental import pallas as pl
+from jax.experimental.pallas import tpu as pltpu
 from jax.sharding import PartitionSpec as P
 
 EPSILON = 1e-06
@@ -265,9 +267,672 @@
     )
 
 
+MESH = pl.DeviceIdType.MESH
+NN = (((1,), (0,)), ((), ()))
+NT = (((1,), (1,)), ((), ()))
+TN = (((0,), (0,)), ((), ()))
+F32 = jnp.float32
+BF16 = jnp.bfloat16
+CHUNKS = 6
+PAD = 208
+BLOCK = 832
+C_A = 0.7978845608
+C_B = 0.7978845608 * 0.044715
+
+
+def dot(left, right, dims=NN):
+    return lax.dot_general(left, right, dims, preferred_element_type=F32)
+
+
+def gelu_and_slope(v):
+    v2 = v * v
+    u = v * (C_B * v2 + C_A)
+    h = 0.5 * jnp.tanh(u) + 0.5
+    act = v * h
+    slope = h + act * (1.0 - h) * ((6.0 * C_B) * v2 + 2.0 * C_A)
+    return act, slope
+
+
+def row_stats(v):
+    centred = v - jnp.mean(v, axis=-1, keepdims=True)
+    spread = jnp.mean(centred * centred, axis=-1, keepdims=True)
+    root = lax.rsqrt(spread + EPSILON)
+    return centred * root, root
+
+
+def mega(
+    counts, tokens, cotangent, pack, weights,
+    block_out, input_grad, grad_shards, small_out, gathered, act_hbm, slope_hbm, mixed_hbm,
+    normed_two, grad_rows, result_acc, grad_two_acc,
+    grads, core_in, cross_out, cross_keep, cross_in, line_out, line_keep, line_in, shards, small_sum,
+    small, tok_in, tok_in_t, tok_out, tok_out_t, vectors, hidden_bias,
+    vector_sums, hidden_sums, tok_in_sum, tok_out_sum,
+    small_sems, z_sems, z_local, x_sems, swap_sems, core_sems, cross_sems, line_sems, end_sems,
+):
+    images, patches, width = tokens.shape
+    hidden = tok_in.shape[0]
+    per_micro = images // counts.shape[1]
+    c = lax.axis_index("dp")
+    f = lax.axis_index("fsdp")
+    zi, qi = f // 4, f % 4
+    partner = (1 - c, f)
+
+    def cross(k):
+        return (c, zi * 4 + (qi ^ k))
+
+    def line(k):
+        return (c, (zi ^ k) * 4 + qi)
+
+    def remote(src, dst, sems, index, device):
+        return pltpu.make_async_remote_copy(
+            src_ref=src, dst_ref=dst, send_sem=sems.at[(0,) + index], recv_sem=sems.at[(1,) + index],
+            device_id=device, device_id_type=MESH,
+        )
+
+    barrier = pltpu.get_barrier_semaphore()
+    for device in [partner] + [cross(k) for k in (1, 2, 3)] + [line(k) for k in (1, 2, 3)]:
+        pl.semaphore_signal(barrier, inc=1, device_id=device, device_id_type=MESH)
+    pl.semaphore_wait(barrier, 7)
+
+    def small_line(k):
+        return remote(small.at[c, zi, qi], small.at[c, zi, qi], small_sems, (k - 1,), line(k))
+
+    def small_cross(k):
+        return remote(small.at[c, :, qi], small.at[c, :, qi], small_sems, (k + 2,), cross(k))
+
+    def small_swap():
+        return remote(small.at[c], small.at[c], small_sems, (6,), partner)
+
+    def z_copy(j, k):
+        return remote(weights.at[c, j], gathered.at[c, j, zi, qi], z_sems, (j, k - 1), line(k))
+
+    def z_own(j):
+        return pltpu.make_async_copy(weights.at[c, j], gathered.at[c, j, zi, qi], z_local.at[j])
+
+    def x_copy(j, k):
+        return remote(gathered.at[c, j, :, qi], gathered.at[c, j, :, qi], x_sems, (j, k - 1), cross(k))
+
+    def swap_copy(j):
+        return remote(gathered.at[c, j], gathered.at[c, j], swap_sems, (j,), partner)
+
+    def x_start(j):
+        for k in (1, 2, 3):
+            z_copy(j, k).wait()
+        z_own(j).wait()
+        for k in (1, 2, 3):
+            x_copy(j, k).start()
+
+    def swap_start(j):
+        for k in (1, 2, 3):
+            x_copy(j, k).wait()
+        swap_copy(j).start()
+
+    def core_copy(p, rows):
+        return remote(
+            grads.at[1 - c, :, :, pl.ds(0, rows)], core_in.at[p, :, :, pl.ds(0, rows)], core_sems, (p,), partner
+        )
+
+    def cross_copy(p, rows, k):
+        return remote(
+            cross_out.at[k - 1, :, pl.ds(0, rows)], cross_in.at[p, k - 1, :, pl.ds(0, rows)],
+            cross_sems, (p, k - 1), cross(k),
+        )
+
+    def line_copy(p, rows, k):
+        return remote(
+            line_out.at[k - 1, pl.ds(0, rows)], line_in.at[p, k - 1, pl.ds(0, rows)], line_sems, (p, k - 1), line(k)
+        )
+
+    def cross_start(p, rows):
+        core_copy(p, rows).wait()
+
+        def per_line(z, carry):
+            for k in range(4):
+                q = qi ^ k
+                total = grads[c, z, q, 0:rows] + core_in[p, z, q, 0:rows]
+                if k == 0:
+                    cross_keep[z, 0:rows] = total
+                else:
+                    cross_out[k - 1, z, 0:rows] = total.astype(BF16)
+            return carry
+
+        lax.fori_loop(0, 4, per_line, 0)
+        for k in (1, 2, 3):
+            cross_copy(p, rows, k).start()
+
+    def line_start(p, rows):
+        for k in (1, 2, 3):
+            cross_copy(p, rows, k).wait()
+        for k in range(4):
+            z = zi ^ k
+            total = cross_keep[z, 0:rows]
+            for m in range(3):
+                total = total + cross_in[p, m, z, 0:rows].astype(F32)
+            if k == 0:
+                line_keep[0:rows] = total
+            else:
+                line_out[k - 1, 0:rows] = total.astype(BF16)
+        for k in (1, 2, 3):
+            line_copy(p, rows, k).start()
+
+    def line_finish(p, rows):
+        for k in (1, 2, 3):
+            line_copy(p, rows, k).wait()
+        total = line_keep[0:rows]
+        for m in range(3):
+            total = total + line_in[p, m, 0:rows].astype(F32)
+        return total
+
+    piece = grads.shape[3]
+
+    small[c, zi, qi] = pack[c]
+    for k in (1, 2, 3):
+        small_line(k).start()
+    for k in (1, 2, 3):
+        small_line(k).wait()
+    for k in (1, 2, 3):
+        small_cross(k).start()
+    for j in range(CHUNKS):
+        z_own(j).start()
+        for k in (1, 2, 3):
+            z_copy(j, k).start()
+    for k in (1, 2, 3):
+        small_cross(k).wait()
+    small_swap().start()
+    small_swap().wait()
+
+    owners = 16
+    part_a = small[0].astype(F32).reshape(owners, 32, 256)
+    part_b = small[1].astype(F32).reshape(owners, 32, 256)
+    full_in = part_a[:, 0:24].reshape(hidden, 256)
+    full_out = part_b[:, 0:24].reshape(hidden, 256)
+    bias_row = pack[1].astype(F32)[24:32]
+    first = lax.broadcasted_iota(jnp.int32, (8, 256), 0) == 0
+    bias_rows = jnp.where(first, bias_row, 0.0)
+    tok_in[...] = full_in.astype(BF16)
+    tok_in_t[...] = jnp.transpose(full_in)[0:PAD].astype(BF16)
+    tok_out[...] = full_out.astype(BF16)
+    out_rows = jnp.concatenate([full_out, bias_rows, jnp.zeros((120, 256), F32)], axis=0)
+    tok_out_t[...] = jnp.transpose(out_rows)[0:PAD].astype(BF16)
+
+    flat_a = part_a.reshape(owners * 32, 256).astype(BF16)
+    pick_r = lax.broadcasted_iota(jnp.int32, (8, owners * 32), 0)
+    pick_p = lax.broadcasted_iota(jnp.int32, (8, owners * 32), 1)
+    pick = jnp.where((pick_p & 31) == 24 + pick_r, 1.0, 0.0).astype(BF16)
+    col = lax.broadcasted_iota(jnp.int32, (256, width), 1)
+    lane = lax.broadcasted_iota(jnp.int32, (256, width), 0)
+    spread = jnp.where(lane == col - 48 * ((col * 43691) >> 21), 1.0, 0.0).astype(BF16)
+    own_n = (lax.broadcasted_iota(jnp.int32, (owners * 32, width), 1) * 43691) >> 21
+    own_p = lax.broadcasted_iota(jnp.int32, (owners * 32, width), 0) >> 5
+    vectors[...] = dot(pick, jnp.where(own_n == own_p, dot(flat_a, spread), 0.0).astype(BF16))
+    span = owners * 32
+    own_n = lax.broadcasted_iota(jnp.int32, (span, span), 1) >> 5
+    own_p = lax.broadcasted_iota(jnp.int32, (span, span), 0) >> 5
+    col = lax.broadcasted_iota(jnp.int32, (256, span), 1)
+    lane = lax.broadcasted_iota(jnp.int32, (256, span), 0)
+    for j in range(CHUNKS):
+        spread = jnp.where(lane == 32 * j + (col & 31), 1.0, 0.0).astype(BF16)
+        rows = dot(pick, jnp.where(own_n == own_p, dot(flat_a, spread), 0.0).astype(BF16))
+        hidden_bias[j] = rows[5:6]
+
+    vector_sums[...] = jnp.zeros(vector_sums.shape, F32)
+    hidden_sums[...] = jnp.zeros(hidden_sums.shape, F32)
+    tok_in_sum[...] = jnp.zeros(tok_in_sum.shape, F32)
+    tok_out_sum[...] = jnp.zeros(tok_out_sum.shape, F32)
+
+    def image_rows(i, count=None):
+        return pl.ds(pl.multiple_of(i * PAD, 16), count or patches)
+
+    def live_of(i):
+        return jnp.where(i % per_micro < counts[0, i // per_micro], 1.0, 0.0).astype(F32)
+
+    def token_forward(x_buf, cot_buf, act_buf, slope_buf, mixed_buf, normed, in_sems, out_sems):
+        def loads(i, slot):
+            return (
+                pltpu.make_async_copy(tokens.at[i], x_buf.at[slot], in_sems.at[slot, 0]),
+                pltpu.make_async_copy(cotangent.at[i], cot_buf.at[slot], in_sems.at[slot, 1]),
+            )
+
+        def stores(i, slot):
+            return (
+                pltpu.make_async_copy(act_buf.at[slot, pl.ds(0, hidden)], act_hbm.at[i], out_sems.at[slot, 0]),
+                pltpu.make_async_copy(slope_buf.at[slot], slope_hbm.at[i], out_sems.at[slot, 1]),
+                pltpu.make_async_copy(mixed_buf.at[slot], mixed_hbm.at[i], out_sems.at[slot, 2]),
+            )
+
+        for copy in loads(0, 0):
+            copy.start()
+        ones_row = lax.broadcasted_iota(jnp.int32, (64, width), 0) == 8
+        normed[192:256] = jnp.where(ones_row, 1.0, 0.0).astype(BF16)
+        ones_row = lax.broadcasted_iota(jnp.int32, (128, width), 0) == 0
+        for slot in range(2):
+            act_buf[slot, hidden : hidden + 128] = jnp.where(ones_row, 1.0, 0.0).astype(BF16)
+
+        def image(i, carry):
+            slot = i % 2
+
+            @pl.when(i + 1 < images)
+            def _():
+                for copy in loads(i + 1, 1 - slot):
+                    copy.start()
+
+            for copy in loads(i, slot):
+                copy.wait()
+
+            @pl.when(i >= 2)
+            def _():
+                for copy in stores(i - 2, slot):
+                    copy.wait()
+
+            @pl.when(i == 2)
+            def _():
+                x_start(0)
+
+            @pl.when(i == 9)
+            def _():
+                swap_start(0)
+                x_start(1)
+
+            x = x_buf[slot].astype(F32)
+            unit, _ = row_stats(x)
+            normed[0:patches] = (unit * vectors[0:1] + vectors[1:2]).astype(BF16)
+            act, slope = gelu_and_slope(dot(tok_in[...], normed[...]))
+            act_buf[slot, 0:hidden] = act.astype(BF16)
+            slope_buf[slot] = slope.astype(BF16)
+            mixed = x + dot(tok_out_t[...], act_buf[slot])[0:patches]
+            mixed_buf[slot] = mixed
+            for copy in stores(i, slot):
+                copy.start()
+            unit, _ = row_stats(mixed)
+            rows = image_rows(i)
+            whole = image_rows(i, PAD)
+            normed_two[whole] = jnp.zeros((PAD, width), BF16)
+            normed_two[rows] = (unit * vectors[2:3] + vectors[3:4]).astype(BF16)
+            grad = cot_buf[slot].astype(F32) * live_of(i)
+            grad_rows[whole] = jnp.zeros((PAD, width), BF16)
+            grad_rows[rows] = grad.astype(BF16)
+            vector_sums[4:5] += jnp.sum(grad, axis=0, keepdims=True)
+            result_acc[whole] = jnp.zeros((PAD, width), F32)
+            result_acc[rows] = mixed + vectors[4:5]
+            grad_two_acc[whole] = jnp.zeros((PAD, width), F32)
+            return carry
+
+        lax.fori_loop(0, images, image, 0)
+        for i in (images - 2, images - 1):
+            for copy in stores(i, i % 2):
+                copy.wait()
+
+    buffers = (
+        pltpu.VMEM((2, patches, width), BF16),
+        pltpu.VMEM((2, patches, width), BF16),
+        pltpu.VMEM((2, hidden + 128, width), BF16),
+        pltpu.VMEM((2, hidden, width), BF16),
+        pltpu.VMEM((2, patches, width), F32),
+        pltpu.VMEM((256, width), BF16),
+    )
+    pl.run_scoped(
+        token_forward, *buffers, pltpu.SemaphoreType.DMA((2, 2)), pltpu.SemaphoreType.DMA((2, 3))
+    )
+
+    def channel(act_all, slope_all, w_in, w_out, load_sems):
+        chunk = w_in.shape[-1]
+
+        def loads(j, p):
+            return [
+                pltpu.make_async_copy(
+                    gathered.at[0, j, :, :, pl.ds(48 * b, 48)], w_in.at[p, :, :, :, pl.ds(256 * b, 256)], load_sems.at[b]
+                )
+                for b in range(2)
+            ] + [
+                pltpu.make_async_copy(
+                    gathered.at[1, j, :, :, pl.ds(32 * b, 32)], w_out.at[p, :, :, :, pl.ds(256 * b, 256)],
+                    load_sems.at[2 + b],
+                )
+                for b in range(3)
+            ]
+
+        swap_copy(0).wait()
+        for copy in loads(0, 0):
+            copy.start()
+        for copy in loads(0, 0):
+            copy.wait()
+
+        def tick(j, carry):
+            p = j % 2
+
+            @pl.when(j >= 1)
+            def _():
+                core_copy(1 - p, piece).start()
+
+            @pl.when(j >= 2)
+            def _():
+                shards[j - 2] = line_finish(p, piece)
+
+            @pl.when(j + 1 < CHUNKS)
+            def _():
+                swap_start(j + 1)
+
+            @pl.when(j < 2)
+            def _():
+                x_start(2 * j + 2)
+                x_start(2 * j + 3)
+
+            def block(b, inner):
+                rows = pl.ds(pl.multiple_of(b * BLOCK, 16), BLOCK)
+                up = w_in[p].reshape(width, chunk)
+                down = w_out[p].reshape(chunk, width)
+                pre = dot(normed_two[rows], up) + hidden_bias[j]
+                grad_act = dot(grad_rows[rows], down, NT)
+                act, slope = gelu_and_slope(pre)
+                grad_pre = grad_act * slope
+                hidden_sums[pl.ds(j, 1)] += jnp.sum(grad_pre, axis=0, keepdims=True)
+                act_all[rows] = act.astype(BF16)
+                slope_all[rows] = grad_pre.astype(BF16)
+                result_acc[rows] += dot(act_all[rows], down)
+                grad_two_acc[rows] += dot(slope_all[rows], up, NT)
+
+                @pl.when((b == 0) & (j >= 1))
+                def _():
+                    cross_start(1 - p, piece)
+
+                @pl.when((b == 1) & (j + 1 < CHUNKS))
+                def _():
+                    swap_copy(j + 1).wait()
+                    for copy in loads(j + 1, 1 - p):
+                        copy.start()
+
+                return inner
+
+            lax.fori_loop(0, normed_two.shape[0] // BLOCK, block, 0)
+            up_grad = dot(normed_two[...], slope_all[...], TN)
+            for b in range(2):
+                grads[0, :, :, 48 * b : 48 * b + 48] = up_grad[:, 256 * b : 256 * b + 256].reshape(4, 4, 48, 256)
+            down_grad = dot(act_all[...], grad_rows[...], TN)
+            for b in range(3):
+                grads[1, :, :, 32 * b : 32 * b + 32] = down_grad[:, 256 * b : 256 * b + 256].reshape(4, 4, 32, 256)
+
+            @pl.when(j >= 1)
+            def _():
+                line_start(1 - p, piece)
+
+            @pl.when(j + 1 < CHUNKS)
+            def _():
+                for copy in loads(j + 1, 1 - p):
+                    copy.wait()
+
+            return carry
+
+        lax.fori_loop(0, CHUNKS, tick, 0)
+
+    total_rows = normed_two.shape[0]
+    pl.run_scoped(
+        channel,
+        pltpu.VMEM((total_rows, 512), BF16),
+        pltpu.VMEM((total_rows, 512), BF16),
+        pltpu.VMEM((2, 4, 4, 48, 512), BF16),
+        pltpu.VMEM((2, 4, 4, 32, 768), BF16),
+        pltpu.SemaphoreType.DMA((5,)),
+    )
+
+    def token_backward(x_buf, out_buf, act_buf, slope_buf, mixed_buf, normed, mixed_low, pre_low, grad_buf, in_sems, out_sems):
+        def loads(i, slot):
+            return (
+                pltpu.make_async_copy(tokens.at[i], x_buf.at[slot], in_sems.at[slot, 0]),
+                pltpu.make_async_copy(act_hbm.at[i], act_buf.at[slot, pl.ds(0, hidden)], in_sems.at[slot, 1]),
+                pltpu.make_async_copy(slope_hbm.at[i], slope_buf.at[slot], in_sems.at[slot, 2]),
+                pltpu.make_async_copy(mixed_hbm.at[i], mixed_buf.at[slot], in_sems.at[slot, 3]),
+            )
+
+        def stores(i, slot):
+            return (
+                pltpu.make_async_copy(out_buf.at[slot], block_out.at[i], out_sems.at[slot, 0]),
+                pltpu.make_async_copy(grad_buf.at[slot], input_grad.at[i], out_sems.at[slot, 1]),
+            )
+
+        for copy in loads(0, 0):
+            copy.start()
+        core_copy(1, piece).start()
+        shards[CHUNKS - 2] = line_finish(0, piece)
+        ones_row = lax.broadcasted_iota(jnp.int32, (64, width), 0) == 8
+        normed[192:256] = jnp.where(ones_row, 1.0, 0.0).astype(BF16)
+        mixed_low[192:256] = jnp.zeros((64, width), BF16)
+        ones_row = lax.broadcasted_iota(jnp.int32, (128, width), 0) == 0
+        for slot in range(2):
+            act_buf[slot, hidden : hidden + 128] = jnp.where(ones_row, 1.0, 0.0).astype(BF16)
+
+        def image(i, carry):
+            slot = i % 2
+
+            @pl.when(i + 1 < images)
+            def _():
+                for copy in loads(i + 1, 1 - slot):
+                    copy.start()
+
+            for copy in loads(i, slot):
+                copy.wait()
+
+            @pl.when(i >= 2)
+            def _():
+                for copy in stores(i - 2, slot):
+                    copy.wait()
+
+            @pl.when(i == 2)
+            def _():
+                cross_start(1, piece)
+
+            @pl.when(i == 8)
+            def _():
+                line_start(1, piece)
+
+            @pl.when(i == 12)
+            def _():
+                shards[CHUNKS - 1] = line_finish(1, piece)
+                shard_swap().start()
+                shard_own().start()
+
+            rows = image_rows(i)
+            unit, root = row_stats(mixed_buf[slot])
+            grad = grad_two_acc[rows]
+            vector_sums[2:3] += jnp.sum(grad * unit, axis=0, keepdims=True)
+            vector_sums[3:4] += jnp.sum(grad, axis=0, keepdims=True)
+            scaled = grad * vectors[2:3]
+            inner = jnp.mean(scaled * unit, axis=-1, keepdims=True)
+            mixed = grad_rows[rows].astype(F32) + root * (
+                scaled - jnp.mean(scaled, axis=-1, keepdims=True) - unit * inner
+            )
+            mixed_low[0:patches] = mixed.astype(BF16)
+            tok_out_sum[...] += dot(act_buf[slot], mixed_low[...], NT)
+            grad_act = dot(tok_out[...], mixed_low[...])
+            pre_low[...] = (grad_act * slope_buf[slot].astype(F32)).astype(BF16)
+            unit, root = row_stats(x_buf[slot].astype(F32))
+            normed[0:patches] = (unit * vectors[0:1] + vectors[1:2]).astype(BF16)
+            tok_in_sum[...] += dot(pre_low[...], normed[...], NT)
+            grad = dot(tok_in_t[...], pre_low[...])[0:patches]
+            vector_sums[0:1] += jnp.sum(grad * unit, axis=0, keepdims=True)
+            vector_sums[1:2] += jnp.sum(grad, axis=0, keepdims=True)
+            scaled = grad * vectors[0:1]
+            inner = jnp.mean(scaled * unit, axis=-1, keepdims=True)
+            grad_buf[slot] = (
+                mixed + root * (scaled - jnp.mean(scaled, axis=-1, keepdims=True) - unit * inner)
+            ).astype(BF16)
+            out_buf[slot] = (result_acc[rows] * live_of(i)).astype(BF16)
+            for copy in stores(i, slot):
+                copy.start()
+            return carry
+
+        lax.fori_loop(0, images, image, 0)
+        for i in (images - 2, images - 1):
+            for copy in stores(i, i % 2):
+                copy.wait()
+
+    def shard_swap():
+        return remote(shards, grad_shards.at[c], end_sems, (0,), partner)
+
+    def shard_own():
+        return pltpu.make_async_copy(shards, grad_shards.at[c], end_sems.at[0, 2])
+
+    pl.run_scoped(
+        token_backward,
+        *buffers,
+        pltpu.VMEM((256, width), BF16),
+        pltpu.VMEM((hidden, width), BF16),
+        pltpu.VMEM((2, patches, width), BF16),
+        pltpu.SemaphoreType.DMA((2, 4)),
+        pltpu.SemaphoreType.DMA((2, 2)),
+    )
+
+    tok_in_rows = tok_in_sum[...].reshape(4, 4, 24, 256)
+    tok_out_rows = tok_out_sum[0:hidden].reshape(4, 4, 24, 256)
+    grads[0, :, :, 0:24] = tok_in_rows
+    grads[1, :, :, 0:24] = tok_out_rows
+    sums = vector_sums[...]
+    hidden_rows = hidden_sums[...]
+    for o in range(owners):
+        grads[0, o // 4, o % 4, 24:32, 0:128] = pltpu.roll(sums, (width - 48 * o) % width, 1)[:, 0:128]
+        grads[0, o // 4, o % 4, 24:32, 128:256] = jnp.zeros((8, 128), F32)
+        grads[0, o // 4, o % 4, 31:32] = tok_out_sum[hidden : hidden + 1]
+        grads[1, o // 4, o % 4, 24:32, 0:128] = pltpu.roll(hidden_rows, (512 - 32 * o) % 512, 1)[:, 0:128]
+        grads[1, o // 4, o % 4, 24:32, 128:256] = jnp.zeros((8, 128), F32)
+    core_copy(0, 32).start()
+    cross_start(0, 32)
+    line_start(0, 32)
+    small_sum[...] = line_finish(0, 32)
+
+    def small_end():
+        return remote(small_sum, small_out.at[c], end_sems, (1,), partner)
+
+    small_own = pltpu.make_async_copy(small_sum, small_out.at[c], end_sems.at[1, 2])
+    small_end().start()
+    small_own.start()
+    small_end().wait()
+    small_own.wait()
+    shard_swap().wait()
+    shard_own().wait()
+
+
+def per_device_fused(
+    tokens, cotangent, counts, ln1_gain, ln1_bias, tok_in, tok_in_bias, tok_out, tok_out_bias,
+    ln2_gain, ln2_bias, ch_in, ch_in_bias, ch_out, ch_out_bias,
+):
+    images, patches, width = tokens.shape
+    per_in, inner = ch_in.shape
+    per_out = ch_out.shape[0]
+    per_tok = tok_in.shape[0]
+    owners = width // per_in
+    hidden = per_tok * owners
+    each = per_out // CHUNKS
+    chunk = each * owners
+
+    def row(vector):
+        return jnp.pad(vector, (0, 256 - vector.shape[0]))[None]
+
+    pad_in = jnp.concatenate(
+        [tok_in, jnp.zeros((per_tok, 4), BF16), tok_in_bias[:, None], jnp.zeros((per_tok, 55), BF16)], axis=1
+    )
+    pad_out = jnp.pad(tok_out, ((0, 0), (0, 256 - patches)))
+    none = jnp.zeros((2, 256), BF16)
+    pack = jnp.stack(
+        [
+            jnp.concatenate(
+                [pad_in, row(ln1_gain), row(ln1_bias), row(ln2_gain), row(ln2_bias), row(ch_out_bias), row(ch_in_bias), none]
+            ),
+            jnp.concatenate([pad_out, row(tok_out_bias), jnp.zeros((7, 256), BF16)]),
+        ]
+    )
+    local_in = ch_in.reshape(per_in, owners, CHUNKS, each).transpose(2, 0, 1, 3).reshape(CHUNKS, per_in, 2, 256)
+    local_in = local_in.transpose(0, 2, 1, 3).reshape(CHUNKS, 96, 256)
+    local_out = ch_out.reshape(CHUNKS, each, 3, 256).transpose(0, 2, 1, 3).reshape(CHUNKS, 96, 256)
+    weights = jnp.stack([local_in, local_out])
+    any_spec = pl.BlockSpec(memory_space=pl.ANY)
+    vmem = pltpu.VMEM
+    dma = pltpu.SemaphoreType.DMA
+    rows = images * PAD
+    shape = jax.ShapeDtypeStruct
+    flops = 12 * rows * width * inner
+    results = pl.pallas_call(
+        mega,
+        in_specs=[
+            pl.BlockSpec(memory_space=pltpu.SMEM), any_spec, any_spec, pl.BlockSpec(memory_space=pltpu.VMEM), any_spec,
+        ],
+        out_specs=[any_spec] * 8,
+        out_shape=[
+            shape(tokens.shape, BF16),
+            shape(tokens.shape, BF16),
+            shape((2, CHUNKS, 96, 256), F32),
+            shape((2, 32, 256), F32),
+            shape((2, CHUNKS, 4, 4, 96, 256), BF16),
+            shape((images, hidden, width), BF16),
+            shape((images, hidden, width), BF16),
+            shape((images, patches, width), F32),
+        ],
+        scratch_shapes=[
+            vmem((rows, width), BF16),
+            vmem((rows, width), BF16),
+            vmem((rows, width), F32),
+            vmem((rows, width), F32),
+            vmem((2, 4, 4, 96, 256), F32),
+            vmem((2, 4, 4, 96, 256), F32),
+            vmem((3, 4, 96, 256), BF16),
+            vmem((4, 96, 256), F32),
+            vmem((2, 3, 4, 96, 256), BF16),
+            vmem((3, 96, 256), BF16),
+            vmem((96, 256), F32),
+            vmem((2, 3, 96, 256), BF16),
+            vmem((CHUNKS, 96, 256), F32),
+            vmem((32, 256), F32),
+            vmem((2, 4, 4, 32, 256), BF16),
+            vmem((hidden, 256), BF16),
+            vmem((PAD, hidden), BF16),
+            vmem((hidden, 256), BF16),
+            vmem((PAD, hidden + 128), BF16),
+            vmem((8, width), F32),
+            vmem((CHUNKS, 1, chunk), F32),
+            vmem((8, width), F32),
+            vmem((8, chunk), F32),
+            vmem((hidden, 256), F32),
+            vmem((hidden + 128, 256), F32),
+            dma((2, 7)),
+            dma((2, CHUNKS, 3)),
+            dma((CHUNKS,)),
+            dma((2, CHUNKS, 3)),
+            dma((2, CHUNKS)),
+            dma((2, 2)),
+            dma((2, 2, 3)),
+            dma((2, 2, 3)),
+            dma((2, 3)),
+        ],
+        compiler_params=pltpu.CompilerParams(
+            collective_id=0, has_side_effects=True, vmem_limit_bytes=61 * 1024 * 1024
+        ),
+        cost_estimate=pl.CostEstimate(flops=flops, bytes_accessed=100_000_000, transcendentals=rows * inner),
+    )(counts, tokens, cotangent, pack, weights)
+    block_out, input_grad, shards, small_sums = results[:4]
+    grad_in = shards[0].reshape(CHUNKS, 2, per_in, 256).transpose(2, 0, 1, 3).reshape(per_in, CHUNKS, owners, each)
+    grad_in = grad_in.transpose(0, 2, 1, 3).reshape(per_in, inner)
+    grad_out = shards[1].reshape(CHUNKS, 3, each, 256).transpose(0, 2, 1, 3).reshape(per_out, width)
+    part_a, part_b = small_sums[0], small_sums[1]
+    return (
+        block_out,
+        input_grad,
+        part_a[24, :per_in],
+        part_a[25, :per_in],
+        part_a[:per_tok, :patches],
+        part_a[:per_tok, 200],
+        part_b[:per_tok, :patches],
+        part_a[31, :patches],
+        part_a[26, :per_in],
+        part_a[27, :per_in],
+        grad_in,
+        part_b[24 : 24 + CHUNKS, :each].reshape(per_out),
+        grad_out,
+        part_a[28, :per_in],
+    )
+
+
 def solution(mesh):
+    fused = mesh.shape["dp"] == 2 and mesh.shape["fsdp"] == 16
     return jax.shard_map(
-        per_device,
+        per_device_fused if fused else per_device,
         mesh=mesh,
         in_specs=(
             P(("dp", "fsdp"), None, None),

time: 950 us -> 283 us (0.30)
  matrix products: 295 us -> 0 us
  waiting for transfers between devices: 279 us -> 0 us
  blocking collectives: 273 us -> 0 us
  Pallas kernels: 0 us -> 236 us
  other arithmetic: 48.3 us -> 3.06 us
  between operations: 19.4 us -> 0.77 us
  local copies, waits for them, and re-layouts: 30.7 us -> 42.9 us
    dot_general x24 -> x0, matrix products: 295 us -> none  [the longest x2 48.6 us: backward(): jnp.einsum('bsd,fd->bsf', grad_out_low, w_down, preferred_element_type=jn...]
    reduce_scatter x4 -> x0, waiting for transfers between devices: 261 us -> none  [the longest x1 126 us: per_device(): lax.psum_scatter(grad_sums[2], 'fsdp', scatter_dimension=0, tiled=True)]
    pallas_call x0 -> x1, Pallas kernels: none -> 236 us  [per_device_fused(): pl.pallas_call(mega, in_specs=[pl.BlockSpec(memory_space=pltpu.SMEM), any...]
    unnamed x2 -> x0, blocking collectives: 153 us -> none
    all_gather x2 -> x0, blocking collectives: 77 us -> none  [the longest x1 39.9 us: per_device(): lax.all_gather(tok_out, 'fsdp', axis=0, tiled=True)]
    psum x2 -> x0, blocking collectives: 43.8 us -> none  [the longest x1 39.1 us: per_device(): shift_total = lax.psum(shift_sum, ('dp', 'fsdp'))]
    reduce_sum x10 -> x0, other arithmetic: 36.7 us -> none  [the longest x4 16.5 us: normalize(): return centred * lax.rsqrt(spread + EPSILON) * gain + shift]
    psum x1 -> x0, waiting for transfers between devices: 16.7 us -> none  [per_device(): lax.psum((grad_sums[0], grad_sums[1], grad_sums[2], grad_sums[3], grad_su...]
  transfers between devices with their start and end apart: 7 -> 0, of which waited for: 4 -> 0; matrix products, arithmetic and copies ran while one was open for 29% -> 0% of each run, Pallas kernels for 0% -> 0%
where the time goes in v1:
time: 283 us; the launch traced here: 282 us
  Pallas kernels  236 us (83%)
  local copies, waits for them, and re-layouts  42.9 us (15%)
  other arithmetic  3.06 us (1%)
    pallas_call x1, Pallas kernels, per_device_fused(): pl.pallas_call(mega, in_specs=[pl.BlockSpec(memory_space=pltpu.SMEM), any...  236 us
    unnamed x15, local copies, waits for them, and re-layouts  26.8 us

profile of v1, /device:TPU:0, one launch (start us, length us, event | category | flops | bytes accessed | tf_op | source)
XLA Modules:
  0.0 282.3 jit_solution(13117958363683282720)
XLA Ops:
  0.6 0.7 pad.28
  1.3 0.7 pad.29
  2.0 0.7 pad.35
  2.6 0.7 pad.30
  3.3 0.7 pad.31
  4.0 0.7 pad.33
  4.7 0.7 pad.32
  5.6 0.7 copy.36
  6.3 0.8 maximum_maximum_fusion
  7.1 0.8 fusion.3
  7.9 0.6 pad_maximum_fusion.1.pack
  8.5 1.1 reshape.51
  9.7 1.3 copy.37
  11.0 1.1 copy.38
  12.1 0.8 reshape.50
  12.9 0.9 pad_maximum_fusion.weights
  13.8 6.7 %copy.41.tokens = bf16[16,196,768]{2,1,0:T(8,128)(2,1)} copy(bf16[16,196,768]{2,0,1:T(8,128)(2,1)} %param.15) | data formatting | bytes 9633792 | tf_op args[0]
  20.5 3.9 %copy.42.cotangent = bf16[16,196,768]{2,1,0:T(8,128)(2,1)} copy(bf16[16,196,768]{2,0,1:T(8,128)(2,1)S(1)} %bitcast.42) | data formatting | bytes 9633792 | tf_op args[1]
  24.4 235.5 %shard_map.254 = (bf16[16,196,768]{2,1,0:T(8,128)(2,1)}, bf16[16,196,768]{2,1,0:T(8,128)(2,1)}, f32[2,6,96,256]{3,2,1,0:T(8,128)}, f32[2,32,256]{2,1,0:T(8,128)}...) custom-call(s32[1,2]{1,0:T(1,128)} %counts.1, ...), custom_call_target="tpu_custom_call" | custom-call | flops 94220845056 | bytes 100000000 | tf_op jit(solution)/shard_map/pallas_call | solution.py:852
  260.0 5.7 %copy.46 = bf16[16,196,768]{2,0,1:T(8,128)(2,1)} copy(bf16[16,196,768]{2,1,0:T(8,128)(2,1)} %get-tuple-element.36) | data formatting | bytes 9633792
  265.6 0.7 slice_reduce_fusion
  266.3 0.6 slice.61
  266.9 0.5 slice_bitcast_fusion.2
  267.4 0.6 slice.58
  268.0 0.6 slice.60
  268.7 0.6 reshape.54
  269.4 0.5 copy.51
  270.3 0.9 copy.49
  271.2 0.9 reshape.52
  272.1 1.9 copy.44
  274.1 2.7 copy.48
  276.7 5.6 %copy.47 = bf16[16,196,768]{2,0,1:T(8,128)(2,1)} copy(bf16[16,196,768]{2,1,0:T(8,128)(2,1)} %get-tuple-element.37) | data formatting | bytes 9633792
  (30 shorter events, 1.0 us)
Async XLA Ops:
  12.9 7.6 %slice-start = ((s8[4816896]{0:T(1024)(128)(4,1)}), s8[4194304]{0:T(1024)(128)(4,1)S(1)}, s32[]{:S(2)}) async-start(s8[4816896]{0:T(1024)(128)(4,1)} %bitcast.41), calls=%async_computation | async-start | bytes 8388608
  13.8 6.7 %slice-start.1 = ((s8[4816896]{0:T(1024)(128)(4,1)}), s8[622592]{0:T(1024)(128)(4,1)S(1)}, s32[]{:S(2)}) async-start(s8[4816896]{0:T(1024)(128)(4,1)} %bitcast.41), calls=%async_computation.1 | async-start | bytes 1245184
  260.0 5.7 %copy-start.1 = (f32[2,32,256]{2,1,0:T(8,128)S(1)}, f32[2,32,256]{2,1,0:T(8,128)}, u32[]{:S(2)}) copy-start(f32[2,32,256]{2,1,0:T(8,128)} %get-tuple-element.20) | copy-start | bytes 196612
  260.0 9.3 %copy-start = (f32[2,6,96,256]{3,2,1,0:T(8,128)S(1)}, f32[2,6,96,256]{3,2,1,0:T(8,128)}, u32[]{:S(2)}) copy-start(f32[2,6,96,256]{3,2,1,0:T(8,128)} %get-tuple-element.21) | copy-start | bytes 3538948

commit v2 on v1

--- a/solution.py
+++ b/solution.py
@@ -274,8 +274,10 @@
 F32 = jnp.float32
 BF16 = jnp.bfloat16
 CHUNKS = 6
-PAD = 208
-BLOCK = 832
+BLOCK = 784
+SPAN = 224
+STEP = 224
+LANES = 128
 C_A = 0.7978845608
 C_B = 0.7978845608 * 0.044715
 
@@ -300,18 +302,30 @@
     return centred * root, root
 
 
+def take(buf, rows):
+    return jnp.concatenate([buf.at[t][rows, :] for t in range(buf.shape[0])], axis=1)
+
+
+def put(buf, rows, value):
+    for t in range(buf.shape[0]):
+        buf.at[t][rows, :] = value[:, LANES * t : LANES * (t + 1)]
+
+
 def mega(
-    counts, tokens, cotangent, pack, weights,
-    block_out, input_grad, grad_shards, small_out, gathered, act_hbm, slope_hbm, mixed_hbm,
+    counts, tokens, cotangent, vector_row, tok_in_own, tok_out_own, ch_in_own, ch_out_own,
+    block_out, input_grad, ch_in_grad, ch_out_grad, small_out, gathered, act_hbm, slope_hbm, mixed_hbm,
     normed_two, grad_rows, result_acc, grad_two_acc,
-    grads, core_in, cross_out, cross_keep, cross_in, line_out, line_keep, line_in, shards, small_sum,
-    small, tok_in, tok_in_t, tok_out, tok_out_t, vectors, hidden_bias,
+    grads, core_in, cross_out, cross_keep, cross_in, line_out, line_keep, line_in, shards, stage_in, stage_out,
+    small_sum, own_weights, small, tok_in, tok_in_t, tok_out, tok_out_t, vectors, hidden_bias,
     vector_sums, hidden_sums, tok_in_sum, tok_out_sum,
     small_sems, z_sems, z_local, x_sems, swap_sems, core_sems, cross_sems, line_sems, end_sems,
 ):
-    images, patches, width = tokens.shape
-    hidden = tok_in.shape[0]
+    total_rows, width = tokens.shape
+    images, hidden = act_hbm.shape[0], act_hbm.shape[1]
+    patches = total_rows // images
     per_micro = images // counts.shape[1]
+    owners = 16
+    tiles = width // LANES
     c = lax.axis_index("dp")
     f = lax.axis_index("fsdp")
     zi, qi = f // 4, f % 4
@@ -332,7 +346,46 @@
     barrier = pltpu.get_barrier_semaphore()
     for device in [partner] + [cross(k) for k in (1, 2, 3)] + [line(k) for k in (1, 2, 3)]:
         pl.semaphore_signal(barrier, inc=1, device_id=device, device_id_type=MESH)
-    pl.semaphore_wait(barrier, 7)
+
+    row = vector_row[...].astype(F32)
+
+    def vector_at(offset, length, lanes=256):
+        moved = row if offset == 0 else pltpu.roll(row, width - offset, 1)
+        lane = lax.broadcasted_iota(jnp.int32, (1, lanes), 1)
+        return jnp.where(lane < length, moved[:, 0:lanes], 0.0)
+
+    lane = lax.broadcasted_iota(jnp.int32, (24, 256), 1)
+    bias_column = jnp.transpose(jnp.broadcast_to(vector_at(240, 24, LANES), (LANES, LANES)))[0:24, 0:1]
+    pad = jnp.zeros((24, 256 - patches), F32)
+    padded = jnp.concatenate([tok_in_own[...].astype(F32), pad], axis=1)
+    padded = jnp.where(lane == 200, jnp.broadcast_to(bias_column, (24, 256)), padded)
+    rows_a = [vector_at(48 * r, 48) for r in range(5)] + [vector_at(264, 192), jnp.zeros((2, 256), F32)]
+    packed_a = jnp.concatenate([padded] + rows_a, axis=0)
+    padded = jnp.concatenate([tok_out_own[...].astype(F32), pad], axis=1)
+    bias_rows = jnp.concatenate([vector_at(456, patches), jnp.zeros((7, 256), F32)], axis=0)
+    packed_b = jnp.concatenate([padded, bias_rows], axis=0)
+    small[c, zi, qi] = jnp.where(c == 0, packed_a, packed_b).astype(BF16)
+
+    @pl.when(c == 0)
+    def _():
+        group = lax.broadcasted_iota(jnp.int32, (48, LANES), 1) >> 5
+        for j in range(CHUNKS):
+            for b in range(2):
+                for t in range(2):
+                    tile = None
+                    for g in range(4):
+                        source = 192 * (8 * b + 4 * t + g) + 32 * j
+                        part = ch_in_own[:, source // LANES * LANES : (source // LANES + 1) * LANES].astype(F32)
+                        shift = (32 * g - source) % LANES
+                        part = part if shift == 0 else pltpu.roll(part, shift, 1)
+                        tile = part if tile is None else jnp.where(group == g, part, tile)
+                    own_weights[j, 48 * b : 48 * b + 48, LANES * t : LANES * (t + 1)] = tile.astype(BF16)
+
+    @pl.when(c == 1)
+    def _():
+        for j in range(CHUNKS):
+            for b in range(3):
+                own_weights[j, 32 * b : 32 * b + 32] = ch_out_own[32 * j : 32 * j + 32, 256 * b : 256 * b + 256]
 
     def small_line(k):
         return remote(small.at[c, zi, qi], small.at[c, zi, qi], small_sems, (k - 1,), line(k))
@@ -344,16 +397,21 @@
         return remote(small.at[c], small.at[c], small_sems, (6,), partner)
 
     def z_copy(j, k):
-        return remote(weights.at[c, j], gathered.at[c, j, zi, qi], z_sems, (j, k - 1), line(k))
+        return remote(own_weights.at[j], gathered.at[c, j, zi, qi], z_sems, (j, k - 1), line(k))
 
     def z_own(j):
-        return pltpu.make_async_copy(weights.at[c, j], gathered.at[c, j, zi, qi], z_local.at[j])
+        return pltpu.make_async_copy(own_weights.at[j], gathered.at[c, j, zi, qi], z_local.at[j])
 
     def x_copy(j, k):
         return remote(gathered.at[c, j, :, qi], gathered.at[c, j, :, qi], x_sems, (j, k - 1), cross(k))
 
     def swap_copy(j):
         return remote(gathered.at[c, j], gathered.at[c, j], swap_sems, (j,), partner)
+
+    def z_start(j):
+        z_own(j).start()
+        for k in (1, 2, 3):
+            z_copy(j, k).start()
 
     def x_start(j):
         for k in (1, 2, 3):
@@ -425,35 +483,83 @@
 
     piece = grads.shape[3]
 
-    small[c, zi, qi] = pack[c]
-    for k in (1, 2, 3):
-        small_line(k).start()
-    for k in (1, 2, 3):
-        small_line(k).wait()
-    for k in (1, 2, 3):
-        small_cross(k).start()
-    for j in range(CHUNKS):
-        z_own(j).start()
+    def live_rows(count):
+        image = lax.broadcasted_iota(jnp.int32, (count, 1), 0) % images
+        live = jnp.zeros((count, 1), F32)
+        for micro in range(counts.shape[1]):
+            inside = (image >= micro * per_micro) & (image < micro * per_micro + counts[0, micro])
+            live = jnp.where(inside, 1.0, live)
+        return live
+
+    def span_rows(b, step=None):
+        if step is None:
+            return pl.ds(pl.multiple_of(b * SPAN, 16), SPAN)
+        return pl.ds(pl.multiple_of(b * SPAN + step * STEP, 16), STEP)
+
+    spans = total_rows // SPAN
+    steps = SPAN // STEP
+
+    def image_rows(i):
+        return pl.ds(i, patches, stride=images)
+
+    def norm_one(x_sems_local):
+        def load(b):
+            return pltpu.make_async_copy(tokens.at[span_rows(b)], normed_two.at[span_rows(b)], x_sems_local.at[b])
+
+        for b in range(spans):
+            load(b).start()
+        pl.semaphore_wait(barrier, 7)
         for k in (1, 2, 3):
-            z_copy(j, k).start()
-    for k in (1, 2, 3):
-        small_cross(k).wait()
-    small_swap().start()
+            small_line(k).start()
+        for j in (0, 1):
+            z_start(j)
+
+        def span(b, carry):
+            load(b).wait()
+
+            def step(s, inner):
+                rows = span_rows(b, s)
+                unit, _ = row_stats(normed_two[rows].astype(F32))
+                put(grad_two_acc, rows, unit)
+                return inner
+
+            lax.fori_loop(0, steps, step, 0)
+
+            @pl.when(b == 5)
+            def _():
+                for k in (1, 2, 3):
+                    small_line(k).wait()
+                for k in (1, 2, 3):
+                    small_cross(k).start()
+
+            @pl.when(b == spans - 1)
+            def _():
+                for k in (1, 2, 3):
+                    small_cross(k).wait()
+                small_swap().start()
+
+            return carry
+
+        lax.fori_loop(0, spans, span, 0)
+
+    pl.run_scoped(norm_one, pltpu.SemaphoreType.DMA((spans,)))
+    cot_copy = pltpu.make_async_copy(cotangent, grad_rows, end_sems.at[0, 2])
+    cot_copy.start()
+    vector_sums[...] = jnp.zeros(vector_sums.shape, F32)
+    hidden_sums[...] = jnp.zeros(hidden_sums.shape, F32)
+    tok_in_sum[...] = jnp.zeros(tok_in_sum.shape, F32)
+    tok_out_sum[...] = jnp.zeros(tok_out_sum.shape, F32)
     small_swap().wait()
 
-    owners = 16
     part_a = small[0].astype(F32).reshape(owners, 32, 256)
     part_b = small[1].astype(F32).reshape(owners, 32, 256)
     full_in = part_a[:, 0:24].reshape(hidden, 256)
     full_out = part_b[:, 0:24].reshape(hidden, 256)
-    bias_row = pack[1].astype(F32)[24:32]
-    first = lax.broadcasted_iota(jnp.int32, (8, 256), 0) == 0
-    bias_rows = jnp.where(first, bias_row, 0.0)
     tok_in[...] = full_in.astype(BF16)
-    tok_in_t[...] = jnp.transpose(full_in)[0:PAD].astype(BF16)
+    tok_in_t[...] = jnp.transpose(full_in).astype(BF16)
     tok_out[...] = full_out.astype(BF16)
     out_rows = jnp.concatenate([full_out, bias_rows, jnp.zeros((120, 256), F32)], axis=0)
-    tok_out_t[...] = jnp.transpose(out_rows)[0:PAD].astype(BF16)
+    tok_out_t[...] = jnp.transpose(out_rows).astype(BF16)
 
     flat_a = part_a.reshape(owners * 32, 256).astype(BF16)
     pick_r = lax.broadcasted_iota(jnp.int32, (8, owners * 32), 0)
@@ -465,113 +571,114 @@
     own_n = (lax.broadcasted_iota(jnp.int32, (owners * 32, width), 1) * 43691) >> 21
     own_p = lax.broadcasted_iota(jnp.int32, (owners * 32, width), 0) >> 5
     vectors[...] = dot(pick, jnp.where(own_n == own_p, dot(flat_a, spread), 0.0).astype(BF16))
-    span = owners * 32
-    own_n = lax.broadcasted_iota(jnp.int32, (span, span), 1) >> 5
-    own_p = lax.broadcasted_iota(jnp.int32, (span, span), 0) >> 5
-    col = lax.broadcasted_iota(jnp.int32, (256, span), 1)
-    lane = lax.broadcasted_iota(jnp.int32, (256, span), 0)
+    span_n = owners * 32
+    own_n = lax.broadcasted_iota(jnp.int32, (span_n, span_n), 1) >> 5
+    own_p = lax.broadcasted_iota(jnp.int32, (span_n, span_n), 0) >> 5
+    col = lax.broadcasted_iota(jnp.int32, (256, span_n), 1)
+    lane = lax.broadcasted_iota(jnp.int32, (256, span_n), 0)
     for j in range(CHUNKS):
         spread = jnp.where(lane == 32 * j + (col & 31), 1.0, 0.0).astype(BF16)
         rows = dot(pick, jnp.where(own_n == own_p, dot(flat_a, spread), 0.0).astype(BF16))
         hidden_bias[j] = rows[5:6]
 
-    vector_sums[...] = jnp.zeros(vector_sums.shape, F32)
-    hidden_sums[...] = jnp.zeros(hidden_sums.shape, F32)
-    tok_in_sum[...] = jnp.zeros(tok_in_sum.shape, F32)
-    tok_out_sum[...] = jnp.zeros(tok_out_sum.shape, F32)
-
-    def image_rows(i, count=None):
-        return pl.ds(pl.multiple_of(i * PAD, 16), count or patches)
-
-    def live_of(i):
-        return jnp.where(i % per_micro < counts[0, i // per_micro], 1.0, 0.0).astype(F32)
-
-    def token_forward(x_buf, cot_buf, act_buf, slope_buf, mixed_buf, normed, in_sems, out_sems):
-        def loads(i, slot):
-            return (
-                pltpu.make_async_copy(tokens.at[i], x_buf.at[slot], in_sems.at[slot, 0]),
-                pltpu.make_async_copy(cotangent.at[i], cot_buf.at[slot], in_sems.at[slot, 1]),
-            )
-
-        def stores(i, slot):
-            return (
-                pltpu.make_async_copy(act_buf.at[slot, pl.ds(0, hidden)], act_hbm.at[i], out_sems.at[slot, 0]),
-                pltpu.make_async_copy(slope_buf.at[slot], slope_hbm.at[i], out_sems.at[slot, 1]),
-                pltpu.make_async_copy(mixed_buf.at[slot], mixed_hbm.at[i], out_sems.at[slot, 2]),
-            )
-
-        for copy in loads(0, 0):
-            copy.start()
+    def ready_tokens(normed, act_buf):
         ones_row = lax.broadcasted_iota(jnp.int32, (64, width), 0) == 8
         normed[192:256] = jnp.where(ones_row, 1.0, 0.0).astype(BF16)
         ones_row = lax.broadcasted_iota(jnp.int32, (128, width), 0) == 0
         for slot in range(2):
             act_buf[slot, hidden : hidden + 128] = jnp.where(ones_row, 1.0, 0.0).astype(BF16)
 
+    def token_forward(act_buf, slope_buf, normed, out_sems, mixed_sems):
+        def stores(i, slot):
+            return (
+                pltpu.make_async_copy(act_buf.at[slot, pl.ds(0, hidden)], act_hbm.at[i], out_sems.at[slot, 0]),
+                pltpu.make_async_copy(slope_buf.at[slot], slope_hbm.at[i], out_sems.at[slot, 1]),
+            )
+
+        ready_tokens(normed, act_buf)
+
         def image(i, carry):
             slot = i % 2
 
-            @pl.when(i + 1 < images)
-            def _():
-                for copy in loads(i + 1, 1 - slot):
-                    copy.start()
-
-            for copy in loads(i, slot):
-                copy.wait()
-
             @pl.when(i >= 2)
             def _():
                 for copy in stores(i - 2, slot):
                     copy.wait()
 
-            @pl.when(i == 2)
+            @pl.when(i == 0)
             def _():
                 x_start(0)
-
-            @pl.when(i == 9)
-            def _():
+                z_start(2)
+
+            @pl.when(i == 6)
+            def _():
+                x_start(1)
+                z_start(3)
                 swap_start(0)
-                x_start(1)
-
-            x = x_buf[slot].astype(F32)
-            unit, _ = row_stats(x)
+
+            @pl.when(i == 12)
+            def _():
+                x_start(2)
+                z_start(4)
+                swap_start(1)
+
+            unit = take(grad_two_acc, image_rows(i))
             normed[0:patches] = (unit * vectors[0:1] + vectors[1:2]).astype(BF16)
             act, slope = gelu_and_slope(dot(tok_in[...], normed[...]))
             act_buf[slot, 0:hidden] = act.astype(BF16)
             slope_buf[slot] = slope.astype(BF16)
-            mixed = x + dot(tok_out_t[...], act_buf[slot])[0:patches]
-            mixed_buf[slot] = mixed
+            put(result_acc, image_rows(i), dot(tok_out_t[...], act_buf[slot])[0:patches])
             for copy in stores(i, slot):
                 copy.start()
-            unit, _ = row_stats(mixed)
-            rows = image_rows(i)
-            whole = image_rows(i, PAD)
-            normed_two[whole] = jnp.zeros((PAD, width), BF16)
-            normed_two[rows] = (unit * vectors[2:3] + vectors[3:4]).astype(BF16)
-            grad = cot_buf[slot].astype(F32) * live_of(i)
-            grad_rows[whole] = jnp.zeros((PAD, width), BF16)
-            grad_rows[rows] = grad.astype(BF16)
-            vector_sums[4:5] += jnp.sum(grad, axis=0, keepdims=True)
-            result_acc[whole] = jnp.zeros((PAD, width), F32)
-            result_acc[rows] = mixed + vectors[4:5]
-            grad_two_acc[whole] = jnp.zeros((PAD, width), F32)
             return carry
 
         lax.fori_loop(0, images, image, 0)
         for i in (images - 2, images - 1):
             for copy in stores(i, i % 2):
                 copy.wait()
-
-    buffers = (
-        pltpu.VMEM((2, patches, width), BF16),
-        pltpu.VMEM((2, patches, width), BF16),
+        cot_copy.wait()
+
+        def mixed_store(b):
+            return pltpu.make_async_copy(
+                result_acc.at[:, span_rows(b)], mixed_hbm.at[:, span_rows(b)], mixed_sems.at[b]
+            )
+
+        live = jnp.broadcast_to(live_rows(STEP), (STEP, width))
+
+        def span(b, carry):
+            def step(s, inner):
+                rows = span_rows(b, s)
+                mixed = normed_two[rows].astype(F32) + take(result_acc, rows)
+                put(result_acc, rows, mixed)
+                unit, _ = row_stats(mixed)
+                normed_two[rows] = (unit * vectors[2:3] + vectors[3:4]).astype(BF16)
+                grad = grad_rows[rows].astype(F32) * live
+                grad_rows[rows] = grad.astype(BF16)
+                put(grad_two_acc, rows, jnp.zeros((STEP, width), F32))
+                return inner + jnp.sum(grad.reshape(STEP // 8, 8, width), axis=0)
+
+            carry = lax.fori_loop(0, steps, step, carry)
+            mixed_store(b).start()
+
+            @pl.when(b == 4)
+            def _():
+                x_start(3)
+                z_start(5)
+
+            return carry
+
+        sums = lax.fori_loop(0, spans, span, jnp.zeros((8, width), F32))
+        vector_sums[4:5] = jnp.sum(sums, axis=0, keepdims=True)
+        for b in range(spans):
+            mixed_store(b).wait()
+
+    pl.run_scoped(
+        token_forward,
         pltpu.VMEM((2, hidden + 128, width), BF16),
         pltpu.VMEM((2, hidden, width), BF16),
-        pltpu.VMEM((2, patches, width), F32),
         pltpu.VMEM((256, width), BF16),
-    )
-    pl.run_scoped(
-        token_forward, *buffers, pltpu.SemaphoreType.DMA((2, 2)), pltpu.SemaphoreType.DMA((2, 3))
+        pltpu.SemaphoreType.DMA((2, 2)),
+        pltpu.SemaphoreType.DMA((spans,)),
     )
 
     def channel(act_all, slope_all, w_in, w_out, load_sems):
@@ -604,19 +711,6 @@
             def _():
                 core_copy(1 - p, piece).start()
 
-            @pl.when(j >= 2)
-            def _():
-                shards[j - 2] = line_finish(p, piece)
-
-            @pl.when(j + 1 < CHUNKS)
-            def _():
-                swap_start(j + 1)
-
-            @pl.when(j < 2)
-            def _():
-                x_start(2 * j + 2)
-                x_start(2 * j + 3)
-
             def block(b, inner):
                 rows = pl.ds(pl.multiple_of(b * BLOCK, 16), BLOCK)
                 up = w_in[p].reshape(width, chunk)
@@ -628,12 +722,29 @@
                 hidden_sums[pl.ds(j, 1)] += jnp.sum(grad_pre, axis=0, keepdims=True)
                 act_all[rows] = act.astype(BF16)
                 slope_all[rows] = grad_pre.astype(BF16)
-                result_acc[rows] += dot(act_all[rows], down)
-                grad_two_acc[rows] += dot(slope_all[rows], up, NT)
+                forward_part = dot(act_all[rows], down)
+                for t in range(tiles):
+                    result_acc[t, rows] += forward_part[:, LANES * t : LANES * (t + 1)]
+                backward_part = dot(slope_all[rows], up, NT)
+                for t in range(tiles):
+                    grad_two_acc[t, rows] += backward_part[:, LANES * t : LANES * (t + 1)]
 
                 @pl.when((b == 0) & (j >= 1))
                 def _():
                     cross_start(1 - p, piece)
+
+                @pl.when((b == 0) & (j == 0))
+                def _():
+                    x_start(4)
+                    swap_start(2)
+
+                @pl.when((b == 2) & (j == 0))
+                def _():
+                    x_start(5)
+
+                @pl.when((b == 2) & (j >= 2))
+                def _():
+                    shards[j - 2] = line_finish(p, piece)
 
                 @pl.when((b == 1) & (j + 1 < CHUNKS))
                 def _():
@@ -641,9 +752,13 @@
                     for copy in loads(j + 1, 1 - p):
                         copy.start()
 
+                @pl.when((b == 3) & (j + 3 < CHUNKS))
+                def _():
+                    swap_start(j + 3)
+
                 return inner
 
-            lax.fori_loop(0, normed_two.shape[0] // BLOCK, block, 0)
+            lax.fori_loop(0, total_rows // BLOCK, block, 0)
             up_grad = dot(normed_two[...], slope_all[...], TN)
             for b in range(2):
                 grads[0, :, :, 48 * b : 48 * b + 48] = up_grad[:, 256 * b : 256 * b + 256].reshape(4, 4, 48, 256)
@@ -664,7 +779,6 @@
 
         lax.fori_loop(0, CHUNKS, tick, 0)
 
-    total_rows = normed_two.shape[0]
     pl.run_scoped(
         channel,
         pltpu.VMEM((total_rows, 512), BF16),
@@ -674,31 +788,107 @@
         pltpu.SemaphoreType.DMA((5,)),
     )
 
-    def token_backward(x_buf, out_buf, act_buf, slope_buf, mixed_buf, normed, mixed_low, pre_low, grad_buf, in_sems, out_sems):
+    def stage_send(stage, out):
+        return remote(stage, out, end_sems, (0,), partner)
+
+    def stage_own(stage, out):
+        return pltpu.make_async_copy(stage, out, end_sems.at[0, 2])
+
+    def send_stages():
+        @pl.when(c == 0)
+        def _():
+            stage_send(stage_in, ch_in_grad).start()
+            stage_own(stage_in, ch_in_grad).start()
+
+        @pl.when(c == 1)
+        def _():
+            stage_send(stage_out, ch_out_grad).start()
+            stage_own(stage_out, ch_out_grad).start()
+
+    def fill_stages():
+        @pl.when(c == 0)
+        def _():
+            group = lax.broadcasted_iota(jnp.int32, (48, LANES), 1) >> 5
+            for t in range(24):
+                tile = None
+                for g in range(4):
+                    unit = LANES * t + 32 * g
+                    o, j = unit // 192, unit % 192 // 32
+                    b, source = o // 8, 32 * (o % 8)
+                    part = shards[j, 48 * b : 48 * b + 48, source // LANES * LANES : (source // LANES + 1) * LANES]
+                    shift = (32 * g - source) % LANES
+                    part = part if shift == 0 else pltpu.roll(part, shift, 1)
+                    tile = part if tile is None else jnp.where(group == g, part, tile)
+                stage_in[:, LANES * t : LANES * (t + 1)] = tile
+
+        @pl.when(c == 1)
+        def _():
+            for j in range(CHUNKS):
+                for b in range(3):
+                    stage_out[32 * j : 32 * j + 32, 256 * b : 256 * b + 256] = shards[j, 32 * b : 32 * b + 32]
+
+    def token_backward(
+        units, mixed_buf, act_buf, slope_buf, normed, mixed_low, pre_low, out_buf, grad_buf, x_sem, in_sems, mixed_sems, out_sems
+    ):
         def loads(i, slot):
             return (
-                pltpu.make_async_copy(tokens.at[i], x_buf.at[slot], in_sems.at[slot, 0]),
-                pltpu.make_async_copy(act_hbm.at[i], act_buf.at[slot, pl.ds(0, hidden)], in_sems.at[slot, 1]),
-                pltpu.make_async_copy(slope_hbm.at[i], slope_buf.at[slot], in_sems.at[slot, 2]),
-                pltpu.make_async_copy(mixed_hbm.at[i], mixed_buf.at[slot], in_sems.at[slot, 3]),
+                pltpu.make_async_copy(act_hbm.at[i], act_buf.at[slot, pl.ds(0, hidden)], in_sems.at[slot, 0]),
+                pltpu.make_async_copy(slope_hbm.at[i], slope_buf.at[slot], in_sems.at[slot, 1]),
             )
 
-        def stores(i, slot):
-            return (
-                pltpu.make_async_copy(out_buf.at[slot], block_out.at[i], out_sems.at[slot, 0]),
-                pltpu.make_async_copy(grad_buf.at[slot], input_grad.at[i], out_sems.at[slot, 1]),
-            )
-
+        def mixed_load(b, slot):
+            return pltpu.make_async_copy(mixed_hbm.at[:, span_rows(b)], mixed_buf.at[slot], mixed_sems.at[slot])
+
+        x_copy_back = pltpu.make_async_copy(tokens, normed_two, x_sem.at[0])
+        mixed_load(0, 0).start()
+        x_copy_back.start()
+        core_copy(1, piece).start()
         for copy in loads(0, 0):
             copy.start()
-        core_copy(1, piece).start()
-        shards[CHUNKS - 2] = line_finish(0, piece)
-        ones_row = lax.broadcasted_iota(jnp.int32, (64, width), 0) == 8
-        normed[192:256] = jnp.where(ones_row, 1.0, 0.0).astype(BF16)
+        ready_tokens(normed, act_buf)
         mixed_low[192:256] = jnp.zeros((64, width), BF16)
-        ones_row = lax.broadcasted_iota(jnp.int32, (128, width), 0) == 0
-        for slot in range(2):
-            act_buf[slot, hidden : hidden + 128] = jnp.where(ones_row, 1.0, 0.0).astype(BF16)
+        x_copy_back.wait()
+
+        def span(b, carry):
+            slot = b % 2
+
+            @pl.when(b + 1 < spans)
+            def _():
+                mixed_load(b + 1, 1 - slot).start()
+
+            mixed_load(b, slot).wait()
+
+            def step(s, sums):
+                rows = span_rows(b, s)
+                inside = pl.ds(pl.multiple_of(s * STEP, 16), STEP)
+                unit, root = row_stats(take(mixed_buf.at[slot], inside))
+                grad = take(grad_two_acc, rows)
+                weighted = grad * unit
+                scaled = grad * vectors[2:3]
+                inner = jnp.mean(scaled * unit, axis=-1, keepdims=True)
+                mixed = grad_rows[rows].astype(F32) + root * (
+                    scaled - jnp.mean(scaled, axis=-1, keepdims=True) - unit * inner
+                )
+                put(grad_two_acc, rows, mixed)
+                unit, _ = row_stats(normed_two[rows].astype(F32))
+                put(units, rows, unit)
+                return (
+                    sums[0] + jnp.sum(weighted.reshape(STEP // 8, 8, width), axis=0),
+                    sums[1] + jnp.sum(grad.reshape(STEP // 8, 8, width), axis=0),
+                )
+
+            carry = lax.fori_loop(0, steps, step, carry)
+
+            @pl.when(b == 6)
+            def _():
+                cross_start(1, piece)
+
+            return carry
+
+        zero = jnp.zeros((8, width), F32)
+        sums = lax.fori_loop(0, spans, span, (zero, zero))
+        vector_sums[2:3] = jnp.sum(sums[0], axis=0, keepdims=True)
+        vector_sums[3:4] = jnp.sum(sums[1], axis=0, keepdims=True)
 
         def image(i, carry):
             slot = i % 2
@@ -711,103 +901,151 @@
             for copy in loads(i, slot):
                 copy.wait()
 
-            @pl.when(i >= 2)
-            def _():
-                for copy in stores(i - 2, slot):
-                    copy.wait()
-
-            @pl.when(i == 2)
-            def _():
-                cross_start(1, piece)
-
-            @pl.when(i == 8)
+            @pl.when(i == 0)
+            def _():
+                shards[CHUNKS - 2] = line_finish(0, piece)
+
+            @pl.when(i == 5)
             def _():
                 line_start(1, piece)
 
-            @pl.when(i == 12)
+            @pl.when(i == 11)
             def _():
                 shards[CHUNKS - 1] = line_finish(1, piece)
-                shard_swap().start()
-                shard_own().start()
+                fill_stages()
+                send_stages()
 
             rows = image_rows(i)
-            unit, root = row_stats(mixed_buf[slot])
-            grad = grad_two_acc[rows]
-            vector_sums[2:3] += jnp.sum(grad * unit, axis=0, keepdims=True)
-            vector_sums[3:4] += jnp.sum(grad, axis=0, keepdims=True)
-            scaled = grad * vectors[2:3]
-            inner = jnp.mean(scaled * unit, axis=-1, keepdims=True)
-            mixed = grad_rows[rows].astype(F32) + root * (
-                scaled - jnp.mean(scaled, axis=-1, keepdims=True) - unit * inner
-            )
-            mixed_low[0:patches] = mixed.astype(BF16)
+            mixed_low[0:patches] = take(grad_two_acc, rows).astype(BF16)
             tok_out_sum[...] += dot(act_buf[slot], mixed_low[...], NT)
             grad_act = dot(tok_out[...], mixed_low[...])
             pre_low[...] = (grad_act * slope_buf[slot].astype(F32)).astype(BF16)
-            unit, root = row_stats(x_buf[slot].astype(F32))
+            unit = take(units, rows)
             normed[0:patches] = (unit * vectors[0:1] + vectors[1:2]).astype(BF16)
             tok_in_sum[...] += dot(pre_low[...], normed[...], NT)
             grad = dot(tok_in_t[...], pre_low[...])[0:patches]
             vector_sums[0:1] += jnp.sum(grad * unit, axis=0, keepdims=True)
             vector_sums[1:2] += jnp.sum(grad, axis=0, keepdims=True)
-            scaled = grad * vectors[0:1]
-            inner = jnp.mean(scaled * unit, axis=-1, keepdims=True)
-            grad_buf[slot] = (
-                mixed + root * (scaled - jnp.mean(scaled, axis=-1, keepdims=True) - unit * inner)
-            ).astype(BF16)
-            out_buf[slot] = (result_acc[rows] * live_of(i)).astype(BF16)
-            for copy in stores(i, slot):
+            put(units, rows, grad)
+            return carry
+
+        lax.fori_loop(0, images, image, 0)
+
+        grads[0, :, :, 0:24] = tok_in_sum[...].reshape(4, 4, 24, 256)
+        grads[1, :, :, 0:24] = tok_out_sum[0:hidden].reshape(4, 4, 24, 256)
+        sums = vector_sums[...]
+        hidden_rows = hidden_sums[...]
+        for o in range(owners):
+            moved = sums if o == 0 else pltpu.roll(sums, width - 48 * o, 1)
+            grads[0, o // 4, o % 4, 24:32, 0:128] = moved[:, 0:128]
+            grads[0, o // 4, o % 4, 24:32, 128:256] = jnp.zeros((8, 128), F32)
+            grads[0, o // 4, o % 4, 31:32] = tok_out_sum[hidden : hidden + 1]
+            moved = hidden_rows if o == 0 else pltpu.roll(hidden_rows, 512 - 32 * o, 1)
+            grads[1, o // 4, o % 4, 24:32, 0:128] = moved[:, 0:128]
+            grads[1, o // 4, o % 4, 24:32, 128:256] = jnp.zeros((8, 128), F32)
+        core_copy(0, 32).start()
+
+        def stores(b, slot):
+            return (
+                pltpu.make_async_copy(out_buf.at[slot], block_out.at[span_rows(b)], out_sems.at[slot, 0]),
+                pltpu.make_async_copy(grad_buf.at[slot], input_grad.at[span_rows(b)], out_sems.at[slot, 1]),
+            )
+
+        live = jnp.broadcast_to(live_rows(STEP), (STEP, width))
+
+        def last(b, carry):
+            slot = b % 2
+
+            @pl.when(b >= 2)
+            def _():
+                for copy in stores(b - 2, slot):
+                    copy.wait()
+
+            def step(s, inner):
+                rows = span_rows(b, s)
+                inside = pl.ds(pl.multiple_of(s * STEP, 16), STEP)
+                unit, root = row_stats(normed_two[rows].astype(F32))
+                scaled = take(units, rows) * vectors[0:1]
+                mean = jnp.mean(scaled * unit, axis=-1, keepdims=True)
+                grad_buf[slot, inside] = (
+                    take(grad_two_acc, rows)
+                    + root * (scaled - jnp.mean(scaled, axis=-1, keepdims=True) - unit * mean)
+                ).astype(BF16)
+                out_buf[slot, inside] = ((take(result_acc, rows) + vectors[4:5]) * live).astype(BF16)
+                return inner
+
+            lax.fori_loop(0, steps, step, 0)
+            for copy in stores(b, slot):
                 copy.start()
+
+            @pl.when(b == 3)
+            def _():
+                cross_start(0, 32)
+
+            @pl.when(b == 11)
+            def _():
+                line_start(0, 32)
+
             return carry
 
-        lax.fori_loop(0, images, image, 0)
-        for i in (images - 2, images - 1):
-            for copy in stores(i, i % 2):
+        lax.fori_loop(0, spans, last, 0)
+        for b in (spans - 2, spans - 1):
+            for copy in stores(b, b % 2):
                 copy.wait()
-
-    def shard_swap():
-        return remote(shards, grad_shards.at[c], end_sems, (0,), partner)
-
-    def shard_own():
-        return pltpu.make_async_copy(shards, grad_shards.at[c], end_sems.at[0, 2])
 
     pl.run_scoped(
         token_backward,
-        *buffers,
+        pltpu.VMEM((tiles, total_rows, LANES), F32),
+        pltpu.VMEM((2, tiles, SPAN, LANES), F32),
+        pltpu.VMEM((2, hidden + 128, width), BF16),
+        pltpu.VMEM((2, hidden, width), BF16),
+        pltpu.VMEM((256, width), BF16),
         pltpu.VMEM((256, width), BF16),
         pltpu.VMEM((hidden, width), BF16),
-        pltpu.VMEM((2, patches, width), BF16),
-        pltpu.SemaphoreType.DMA((2, 4)),
+        pltpu.VMEM((2, SPAN, width), BF16),
+        pltpu.VMEM((2, SPAN, width), BF16),
+        pltpu.SemaphoreType.DMA((1,)),
         pltpu.SemaphoreType.DMA((2, 2)),
-    )
-
-    tok_in_rows = tok_in_sum[...].reshape(4, 4, 24, 256)
-    tok_out_rows = tok_out_sum[0:hidden].reshape(4, 4, 24, 256)
-    grads[0, :, :, 0:24] = tok_in_rows
-    grads[1, :, :, 0:24] = tok_out_rows
-    sums = vector_sums[...]
-    hidden_rows = hidden_sums[...]
-    for o in range(owners):
-        grads[0, o // 4, o % 4, 24:32, 0:128] = pltpu.roll(sums, (width - 48 * o) % width, 1)[:, 0:128]
-        grads[0, o // 4, o % 4, 24:32, 128:256] = jnp.zeros((8, 128), F32)
-        grads[0, o // 4, o % 4, 31:32] = tok_out_sum[hidden : hidden + 1]
-        grads[1, o // 4, o % 4, 24:32, 0:128] = pltpu.roll(hidden_rows, (512 - 32 * o) % 512, 1)[:, 0:128]
-        grads[1, o // 4, o % 4, 24:32, 128:256] = jnp.zeros((8, 128), F32)
-    core_copy(0, 32).start()
-    cross_start(0, 32)
-    line_start(0, 32)
+        pltpu.SemaphoreType.DMA((2,)),
+        pltpu.SemaphoreType.DMA((2, 2)),
+    )
+
     small_sum[...] = line_finish(0, 32)
-
-    def small_end():
-        return remote(small_sum, small_out.at[c], end_sems, (1,), partner)
-
+    small_end = remote(small_sum, small_out.at[c], end_sems, (1,), partner)
     small_own = pltpu.make_async_copy(small_sum, small_out.at[c], end_sems.at[1, 2])
-    small_end().start()
+    small_end.start()
     small_own.start()
-    small_end().wait()
+    small_end.wait()
     small_own.wait()
-    shard_swap().wait()
-    shard_own().wait()
+
+    @pl.when(c == 0)
+    def _():
+        stage_send(stage_in, ch_in_grad).wait_send()
+        stage_own(stage_in, ch_in_grad).wait()
+        stage_send(stage_out, ch_out_grad).wait_recv()
+
+    @pl.when(c == 1)
+    def _():
+        stage_send(stage_out, ch_out_grad).wait_send()
+        stage_own(stage_out, ch_out_grad).wait()
+        stage_send(stage_in, ch_in_grad).wait_recv()
+
+
+def finish(small, ch_in_sum, ch_out_sum, *outs):
+    gain_one, bias_one, tok_in, tok_in_bias, tok_out, tok_out_bias, gain_two, bias_two, ch_in, ch_in_bias, ch_out, ch_out_bias = outs
+    per_tok, patches = tok_in.shape
+    ch_in[...] = ch_in_sum[...]
+    ch_out[...] = ch_out_sum[...]
+    tok_in[...] = small[0, 0:per_tok, 0:patches]
+    tok_out[...] = small[1, 0:per_tok, 0:patches]
+    column = jnp.broadcast_to(small[0, 0:32, 200:201], (32, LANES))
+    flipped = jnp.transpose(jnp.concatenate([column, jnp.zeros((LANES - 32, LANES), F32)], axis=0))
+    tok_in_bias[...] = flipped[0:1, 0:per_tok]
+    tok_out_bias[...] = small[0, 31:32, 0:patches]
+    for r, out in enumerate((gain_one, bias_one, gain_two, bias_two, ch_out_bias)):
+        out[...] = small[0, 24 + r : 25 + r, 0 : out.shape[1]]
+    for j in range(CHUNKS):
+        ch_in_bias[j : j + 1] = small[1, 24 + j : 25 + j, 0 : ch_in_bias.shape[1]]
 
 
 def per_device_fused(
@@ -822,54 +1060,41 @@
     hidden = per_tok * owners
     each = per_out // CHUNKS
     chunk = each * owners
-
-    def row(vector):
-        return jnp.pad(vector, (0, 256 - vector.shape[0]))[None]
-
-    pad_in = jnp.concatenate(
-        [tok_in, jnp.zeros((per_tok, 4), BF16), tok_in_bias[:, None], jnp.zeros((per_tok, 55), BF16)], axis=1
-    )
-    pad_out = jnp.pad(tok_out, ((0, 0), (0, 256 - patches)))
-    none = jnp.zeros((2, 256), BF16)
-    pack = jnp.stack(
-        [
-            jnp.concatenate(
-                [pad_in, row(ln1_gain), row(ln1_bias), row(ln2_gain), row(ln2_bias), row(ch_out_bias), row(ch_in_bias), none]
-            ),
-            jnp.concatenate([pad_out, row(tok_out_bias), jnp.zeros((7, 256), BF16)]),
-        ]
-    )
-    local_in = ch_in.reshape(per_in, owners, CHUNKS, each).transpose(2, 0, 1, 3).reshape(CHUNKS, per_in, 2, 256)
-    local_in = local_in.transpose(0, 2, 1, 3).reshape(CHUNKS, 96, 256)
-    local_out = ch_out.reshape(CHUNKS, each, 3, 256).transpose(0, 2, 1, 3).reshape(CHUNKS, 96, 256)
-    weights = jnp.stack([local_in, local_out])
+    rows = images * patches
+
+    def by_patch(array):
+        return array.transpose(1, 0, 2).reshape(rows, width)
+
+    vector_row = jnp.concatenate(
+        [ln1_gain, ln1_bias, ln2_gain, ln2_bias, ch_out_bias, tok_in_bias, ch_in_bias, tok_out_bias]
+    )
+    vector_row = jnp.pad(vector_row, (0, width - vector_row.shape[0]))[None]
     any_spec = pl.BlockSpec(memory_space=pl.ANY)
+    vmem_spec = pl.BlockSpec(memory_space=pltpu.VMEM)
     vmem = pltpu.VMEM
     dma = pltpu.SemaphoreType.DMA
-    rows = images * PAD
     shape = jax.ShapeDtypeStruct
-    flops = 12 * rows * width * inner
+    tiled = (width // LANES, rows, LANES)
     results = pl.pallas_call(
         mega,
-        in_specs=[
-            pl.BlockSpec(memory_space=pltpu.SMEM), any_spec, any_spec, pl.BlockSpec(memory_space=pltpu.VMEM), any_spec,
-        ],
-        out_specs=[any_spec] * 8,
+        in_specs=[pl.BlockSpec(memory_space=pltpu.SMEM), any_spec, any_spec] + [vmem_spec] * 5,
+        out_specs=[any_spec] * 9,
         out_shape=[
-            shape(tokens.shape, BF16),
-            shape(tokens.shape, BF16),
-            shape((2, CHUNKS, 96, 256), F32),
+            shape((rows, width), BF16),
+            shape((rows, width), BF16),
+            shape(ch_in.shape, F32),
+            shape(ch_out.shape, F32),
             shape((2, 32, 256), F32),
             shape((2, CHUNKS, 4, 4, 96, 256), BF16),
             shape((images, hidden, width), BF16),
             shape((images, hidden, width), BF16),
-            shape((images, patches, width), F32),
+            shape(tiled, F32),
         ],
         scratch_shapes=[
             vmem((rows, width), BF16),
             vmem((rows, width), BF16),
-            vmem((rows, width), F32),
-            vmem((rows, width), F32),
+            vmem(tiled, F32),
+            vmem(tiled, F32),
             vmem((2, 4, 4, 96, 256), F32),
             vmem((2, 4, 4, 96, 256), F32),
             vmem((3, 4, 96, 256), BF16),
@@ -879,12 +1104,15 @@
             vmem((96, 256), F32),
             vmem((2, 3, 96, 256), BF16),
             vmem((CHUNKS, 96, 256), F32),
+            vmem(ch_in.shape, F32),
+            vmem(ch_out.shape, F32),
             vmem((32, 256), F32),
+            vmem((CHUNKS, 96, 256), BF16),
             vmem((2, 4, 4, 32, 256), BF16),
             vmem((hidden, 256), BF16),
-            vmem((PAD, hidden), BF16),
+            vmem((256, hidden), BF16),
             vmem((hidden, 256), BF16),
-            vmem((PAD, hidden + 128), BF16),
+            vmem((256, hidden + 128), BF16),
             vmem((8, width), F32),
             vmem((CHUNKS, 1, chunk), F32),
             vmem((8, width), F32),
@@ -904,29 +1132,29 @@
         compiler_params=pltpu.CompilerParams(
             collective_id=0, has_side_effects=True, vmem_limit_bytes=61 * 1024 * 1024
         ),
-        cost_estimate=pl.CostEstimate(flops=flops, bytes_accessed=100_000_000, transcendentals=rows * inner),
-    )(counts, tokens, cotangent, pack, weights)
-    block_out, input_grad, shards, small_sums = results[:4]
-    grad_in = shards[0].reshape(CHUNKS, 2, per_in, 256).transpose(2, 0, 1, 3).reshape(per_in, CHUNKS, owners, each)
-    grad_in = grad_in.transpose(0, 2, 1, 3).reshape(per_in, inner)
-    grad_out = shards[1].reshape(CHUNKS, 3, each, 256).transpose(0, 2, 1, 3).reshape(per_out, width)
-    part_a, part_b = small_sums[0], small_sums[1]
-    return (
-        block_out,
-        input_grad,
-        part_a[24, :per_in],
-        part_a[25, :per_in],
-        part_a[:per_tok, :patches],
-        part_a[:per_tok, 200],
-        part_b[:per_tok, :patches],
-        part_a[31, :patches],
-        part_a[26, :per_in],
-        part_a[27, :per_in],
-        grad_in,
-        part_b[24 : 24 + CHUNKS, :each].reshape(per_out),
-        grad_out,
-        part_a[28, :per_in],
-    )
+        cost_estimate=pl.CostEstimate(
+            flops=12 * rows * width * inner, bytes_accessed=100_000_000, transcendentals=rows * inner
+        ),
+    )(counts, by_patch(tokens), by_patch(cotangent), vector_row, tok_in, tok_out, ch_in, ch_out)
+    block_out, input_grad, in_sum, out_sum, small = results[:5]
+    line = shape((1, per_in), F32)
+    outs = pl.pallas_call(
+        finish,
+        in_specs=[vmem_spec] * 3,
+        out_specs=[vmem_spec] * 12,
+        out_shape=[
+            line, line, shape(tok_in.shape, F32), shape((1, per_tok), F32), shape(tok_out.shape, F32),
+            shape((1, patches), F32), line, line, shape(ch_in.shape, F32), shape((CHUNKS, each), F32),
+            shape(ch_out.shape, F32), line,
+        ],
+    )(small, in_sum, out_sum)
+
+    def by_image(array):
+        return array.reshape(patches, images, width).transpose(1, 0, 2)
+
+    flat = (0, 1, 3, 5, 6, 7, 9, 11)
+    outs = [out.reshape(-1) if n in flat else out for n, out in enumerate(outs)]
+    return (by_image(block_out), by_image(input_grad), *outs)
 
 
 def solution(mesh):

time: 283 us -> 237 us (0.84)
  local copies, waits for them, and re-layouts: 42.9 us -> 14.6 us
  Pallas kernels: 236 us -> 221 us
  other arithmetic: 3.06 us -> 0.01 us
    unnamed x15 -> x6, local copies, waits for them, and re-layouts: 26.8 us -> 7.28 us
    pallas_call x1, Pallas kernels: 236 us -> 219 us  [per_device_fused(): pl.pallas_call(mega, in_specs=[pl.BlockSpec(memory_space=pltpu.SMEM), any...]
    concatenate x4 -> x1, local copies, waits for them, and re-layouts: 0.26 us -> 5.43 us  [per_device_fused(): jnp.concatenate([ln1_gain, ln1_bias, ln2_gain, ln2_bias, ch_out_bias, tok...]
    pad x7 -> x1, local copies, waits for them, and re-layouts: 4.62 us -> 0.01 us  [per_device_fused(): vector_row = jnp.pad(vector_row, (0, width - vector_row.shape[0]))[None]]
    transpose x4 -> x0, local copies, waits for them, and re-layouts: 3.08 us -> none  [the longest x1 1.93 us: per_device_fused(): grad_in = grad_in.transpose(0, 2, 1, 3).reshape(per_in, inner)]
where the time goes in v2:
time: 237 us; the launch traced here: 236 us
  Pallas kernels  221 us (93%)
  local copies, waits for them, and re-layouts  14.6 us (6%)
    pallas_call x1, Pallas kernels, per_device_fused(): pl.pallas_call(mega, in_specs=[pl.BlockSpec(memory_space=pltpu.SMEM), any...  219 us
    unnamed x6, local copies, waits for them, and re-layouts  7.28 us
    concatenate x1, local copies, waits for them, and re-layouts, per_device_fused(): jnp.concatenate([ln1_gain, ln1_bias, ln2_gain, ln2_bias, ch_out_bias, tok...  5.43 us

profile of v2, /device:TPU:0, one launch (start us, length us, event | category | flops | bytes accessed | tf_op | source)
XLA Modules:
  0.0 236.5 jit_solution(16292563444695823942)
XLA Ops:
  0.6 5.4 %concatenate.3 = bf16[652]{0:T(1024)(128)(2,1)S(1)} concatenate(bf16[48]{0:T(256)(128)(2,1)} %param.18, bf16[48]{0:T(256)(128)(2,1)} %param.19, bf16[48]{0:T(256)(128)(2,1)} %param.24, bf16[48]{0:T(256)(128)(2,1)} %param.25, bf16[48]{0:T(256)(128)(2,1)} %param.29, bf16[24]{0:T(256)(128)(2,1)} %param.21, bf16[192]{0:T(256)(128)(2,1)} %param.27, bf16[196]{0:T(256)(128)(2,1)} %param.23), dimensions={0} | concatenate | bytes 2608 | tf_op jit(solution)/shard_map/concatenate | solution.py:1068
  6.1 0.6 broadcast_in_dim.3.vector_row
  6.7 218.7 %shard_map.254 = (bf16[3136,768]{1,0:T(8,128)(2,1)}, bf16[3136,768]{1,0:T(8,128)(2,1)}, f32[48,3072]{1,0:T(8,128)}, f32[192,768]{1,0:T(8,128)}, f32[2,32,256]{2,...) custom-call(s32[1,2]{1,0:T(1,128)} %counts.1, ...), custom_call_target="tpu_custom_call" | custom-call | flops 88785027072 | bytes 100000000 | tf_op jit(solution)/shard_map/pallas_call | solution.py:1078
  225.4 0.0 slice-start
  225.4 2.4 %shard_map.255 = (f32[1,48]{1,0:T(1,128)}, f32[1,48]{1,0:T(1,128)}, f32[24,196]{1,0:T(8,128)}, f32[1,24]{1,0:T(1,128)}, f32[24,196]{1,0:T(8,128)}, /*index=5*/f3...) custom-call(f32[2,32,256]{2,1,0:T(8,128)} %get-tuple-element.33.smal, ...), custom_call_target="tpu_custom_call" | custom-call | tf_op jit(solution)/shard_map/pallas_call | solution.py:1141
  227.8 1.3 reshape.74
  229.2 0.0 slice-start.1
  229.2 5.1 %copy.31 = bf16[16,196,768]{2,0,1:T(8,128)(2,1)} copy(bf16[16,196,768]{2,0,1:T(8,128)(2,1)} %bitcast.22) | data formatting | bytes 9633792
  234.2 0.0 slice-done
  234.2 0.0 slice-done.1
  234.2 2.2 copy.32
  (2 shorter events, 0.0 us)
Async XLA Ops:
  225.4 8.8 %slice-start = ((s8[4816896]{0:T(1024)(128)(4,1)}), s8[622592]{0:T(1024)(128)(4,1)S(1)}, s32[]{:S(2)}) async-start(s8[4816896]{0:T(1024)(128)(4,1)} %bitcast.19), calls=%async_computation | async-start | bytes 1245184
  229.2 5.1 %slice-start.1 = ((s8[4816896]{0:T(1024)(128)(4,1)}), s8[4194304]{0:T(1024)(128)(4,1)S(1)}, s32[]{:S(2)}) async-start(s8[4816896]{0:T(1024)(128)(4,1)} %bitcast.19), calls=%async_computation.1 | async-start | bytes 8388608

commit v3 on v2

--- a/solution.py
+++ b/solution.py
@@ -276,7 +276,6 @@
 CHUNKS = 6
 BLOCK = 784
 SPAN = 224
-STEP = 224
 LANES = 128
 C_A = 0.7978845608
 C_B = 0.7978845608 * 0.044715
@@ -287,35 +286,36 @@
 
 
 def gelu_and_slope(v):
-    v2 = v * v
-    u = v * (C_B * v2 + C_A)
-    h = 0.5 * jnp.tanh(u) + 0.5
+    ratio = C_B * (v * v) + C_A
+    t = jnp.tanh(v * ratio)
+    h = 0.5 * t + 0.5
     act = v * h
-    slope = h + act * (1.0 - h) * ((6.0 * C_B) * v2 + 2.0 * C_A)
+    slope = h + act * (1.0 - t) * (3.0 * ratio - 2.0 * C_A)
     return act, slope
 
 
 def row_stats(v):
-    centred = v - jnp.mean(v, axis=-1, keepdims=True)
+    mean = jnp.mean(v, axis=-1, keepdims=True)
+    centred = v - mean
     spread = jnp.mean(centred * centred, axis=-1, keepdims=True)
     root = lax.rsqrt(spread + EPSILON)
-    return centred * root, root
-
-
-def take(buf, rows):
-    return jnp.concatenate([buf.at[t][rows, :] for t in range(buf.shape[0])], axis=1)
+    return centred * root, root, mean
+
+
+def take(buf, rows, count=6):
+    return jnp.concatenate([buf.at[t][rows, :] for t in range(count)], axis=1)
 
 
 def put(buf, rows, value):
-    for t in range(buf.shape[0]):
+    for t in range(value.shape[1] // LANES):
         buf.at[t][rows, :] = value[:, LANES * t : LANES * (t + 1)]
 
 
 def mega(
     counts, tokens, cotangent, vector_row, tok_in_own, tok_out_own, ch_in_own, ch_out_own,
-    block_out, input_grad, ch_in_grad, ch_out_grad, small_out, gathered, act_hbm, slope_hbm, mixed_hbm,
-    normed_two, grad_rows, result_acc, grad_two_acc,
-    grads, core_in, cross_out, cross_keep, cross_in, line_out, line_keep, line_in, shards, stage_in, stage_out,
+    block_out, input_grad, ch_in_grad, ch_out_grad, small_out, gathered, act_hbm, slope_hbm, unit_two_hbm,
+    normed_two, grad_rows, result_acc, grad_two_acc, stats,
+    grads, core_in, cross_out, cross_keep, cross_in, line_out, line_keep, line_in, shards, stage_in,
     small_sum, own_weights, small, tok_in, tok_in_t, tok_out, tok_out_t, vectors, hidden_bias,
     vector_sums, hidden_sums, tok_in_sum, tok_out_sum,
     small_sems, z_sems, z_local, x_sems, swap_sems, core_sems, cross_sems, line_sems, end_sems,
@@ -366,27 +366,6 @@
     packed_b = jnp.concatenate([padded, bias_rows], axis=0)
     small[c, zi, qi] = jnp.where(c == 0, packed_a, packed_b).astype(BF16)
 
-    @pl.when(c == 0)
-    def _():
-        group = lax.broadcasted_iota(jnp.int32, (48, LANES), 1) >> 5
-        for j in range(CHUNKS):
-            for b in range(2):
-                for t in range(2):
-                    tile = None
-                    for g in range(4):
-                        source = 192 * (8 * b + 4 * t + g) + 32 * j
-                        part = ch_in_own[:, source // LANES * LANES : (source // LANES + 1) * LANES].astype(F32)
-                        shift = (32 * g - source) % LANES
-                        part = part if shift == 0 else pltpu.roll(part, shift, 1)
-                        tile = part if tile is None else jnp.where(group == g, part, tile)
-                    own_weights[j, 48 * b : 48 * b + 48, LANES * t : LANES * (t + 1)] = tile.astype(BF16)
-
-    @pl.when(c == 1)
-    def _():
-        for j in range(CHUNKS):
-            for b in range(3):
-                own_weights[j, 32 * b : 32 * b + 32] = ch_out_own[32 * j : 32 * j + 32, 256 * b : 256 * b + 256]
-
     def small_line(k):
         return remote(small.at[c, zi, qi], small.at[c, zi, qi], small_sems, (k - 1,), line(k))
 
@@ -483,69 +462,102 @@
 
     piece = grads.shape[3]
 
-    def live_rows(count):
-        image = lax.broadcasted_iota(jnp.int32, (count, 1), 0) % images
-        live = jnp.zeros((count, 1), F32)
+    def live_rows():
+        image = lax.broadcasted_iota(jnp.int32, (images, 1), 0)
+        live = jnp.zeros((images, 1), F32)
         for micro in range(counts.shape[1]):
             inside = (image >= micro * per_micro) & (image < micro * per_micro + counts[0, micro])
             live = jnp.where(inside, 1.0, live)
-        return live
-
-    def span_rows(b, step=None):
-        if step is None:
-            return pl.ds(pl.multiple_of(b * SPAN, 16), SPAN)
-        return pl.ds(pl.multiple_of(b * SPAN + step * STEP, 16), STEP)
+        return jnp.broadcast_to(live, (images, width))
+
+    def masked(value, live):
+        return (value.reshape(SPAN // images, images, width) * live[None]).reshape(SPAN, width)
+
+    def row_sum(value):
+        return jnp.sum(value.reshape(4, SPAN // 32, 8, width).sum(1), axis=0)
+
+    stat_lane = lax.broadcasted_iota(jnp.int32, (SPAN, LANES), 1)
+
+    def span_rows(b):
+        return pl.ds(pl.multiple_of(b * SPAN, 16), SPAN)
 
     spans = total_rows // SPAN
-    steps = SPAN // STEP
 
     def image_rows(i):
         return pl.ds(i, patches, stride=images)
 
-    def norm_one(x_sems_local):
-        def load(b):
-            return pltpu.make_async_copy(tokens.at[span_rows(b)], normed_two.at[span_rows(b)], x_sems_local.at[b])
+    def own_rows():
+        @pl.when(c == 0)
+        def _():
+            group = lax.broadcasted_iota(jnp.int32, (48, LANES), 1) >> 5
+            for j in range(CHUNKS):
+                for b in range(2):
+                    for t in range(2):
+                        tile = None
+                        for g in range(4):
+                            source = 192 * (8 * b + 4 * t + g) + 32 * j
+                            part = ch_in_own[:, source // LANES * LANES : (source // LANES + 1) * LANES].astype(F32)
+                            shift = (32 * g - source) % LANES
+                            part = part if shift == 0 else pltpu.roll(part, shift, 1)
+                            tile = part if tile is None else jnp.where(group == g, part, tile)
+                        own_weights[j, 48 * b : 48 * b + 48, LANES * t : LANES * (t + 1)] = tile.astype(BF16)
+
+        @pl.when(c == 1)
+        def _():
+            for j in range(CHUNKS):
+                for b in range(3):
+                    own_weights[j, 32 * b : 32 * b + 32] = ch_out_own[32 * j : 32 * j + 32, 256 * b : 256 * b + 256]
+
+    def norm_one(load_sems):
+        def loads(b):
+            return (
+                pltpu.make_async_copy(tokens.at[span_rows(b)], normed_two.at[span_rows(b)], load_sems.at[0, b]),
+                pltpu.make_async_copy(cotangent.at[span_rows(b)], grad_rows.at[span_rows(b)], load_sems.at[1, b]),
+            )
 
         for b in range(spans):
-            load(b).start()
+            for copy in loads(b):
+                copy.start()
         pl.semaphore_wait(barrier, 7)
         for k in (1, 2, 3):
             small_line(k).start()
-        for j in (0, 1):
-            z_start(j)
+        own_rows()
+        z_start(0)
+        live = live_rows()
 
         def span(b, carry):
-            load(b).wait()
-
-            def step(s, inner):
-                rows = span_rows(b, s)
-                unit, _ = row_stats(normed_two[rows].astype(F32))
-                put(grad_two_acc, rows, unit)
-                return inner
-
-            lax.fori_loop(0, steps, step, 0)
-
-            @pl.when(b == 5)
+            for copy in loads(b):
+                copy.wait()
+            rows = span_rows(b)
+            unit, root, mean = row_stats(normed_two[rows].astype(F32))
+            put(grad_two_acc, rows, unit)
+            stats[rows] = jnp.where(stat_lane < 32, root, mean)
+            grad = masked(grad_rows[rows].astype(F32), live)
+            grad_rows[rows] = grad.astype(BF16)
+
+            @pl.when(b == 4)
             def _():
                 for k in (1, 2, 3):
                     small_line(k).wait()
                 for k in (1, 2, 3):
                     small_cross(k).start()
-
-            @pl.when(b == spans - 1)
+                z_start(1)
+
+            @pl.when(b == 10)
             def _():
                 for k in (1, 2, 3):
                     small_cross(k).wait()
                 small_swap().start()
 
-            return carry
-
-        lax.fori_loop(0, spans, span, 0)
-
-    pl.run_scoped(norm_one, pltpu.SemaphoreType.DMA((spans,)))
-    cot_copy = pltpu.make_async_copy(cotangent, grad_rows, end_sems.at[0, 2])
-    cot_copy.start()
-    vector_sums[...] = jnp.zeros(vector_sums.shape, F32)
+            return carry + row_sum(grad)
+
+        sums = lax.fori_loop(0, spans, span, jnp.zeros((8, width), F32))
+        vector_sums[...] = jnp.zeros(vector_sums.shape, F32)
+        vector_sums[4:5] = jnp.sum(sums, axis=0, keepdims=True)
+    pl.run_scoped(
+        norm_one,
+        pltpu.SemaphoreType.DMA((2, spans)),
+    )
     hidden_sums[...] = jnp.zeros(hidden_sums.shape, F32)
     tok_in_sum[...] = jnp.zeros(tok_in_sum.shape, F32)
     tok_out_sum[...] = jnp.zeros(tok_out_sum.shape, F32)
@@ -581,104 +593,103 @@
         rows = dot(pick, jnp.where(own_n == own_p, dot(flat_a, spread), 0.0).astype(BF16))
         hidden_bias[j] = rows[5:6]
 
-    def ready_tokens(normed, act_buf):
-        ones_row = lax.broadcasted_iota(jnp.int32, (64, width), 0) == 8
-        normed[192:256] = jnp.where(ones_row, 1.0, 0.0).astype(BF16)
-        ones_row = lax.broadcasted_iota(jnp.int32, (128, width), 0) == 0
-        for slot in range(2):
-            act_buf[slot, hidden : hidden + 128] = jnp.where(ones_row, 1.0, 0.0).astype(BF16)
-
-    def token_forward(act_buf, slope_buf, normed, out_sems, mixed_sems):
+    ones_low = jnp.where(lax.broadcasted_iota(jnp.int32, (64, width), 0) == 8, 1.0, 0.0).astype(BF16)
+    ones_act = jnp.where(lax.broadcasted_iota(jnp.int32, (128, width), 0) == 0, 1.0, 0.0).astype(BF16)
+
+    def token_forward(act_buf, slope_buf, normed, unit_buf, out_sems, unit_sems):
         def stores(i, slot):
             return (
                 pltpu.make_async_copy(act_buf.at[slot, pl.ds(0, hidden)], act_hbm.at[i], out_sems.at[slot, 0]),
                 pltpu.make_async_copy(slope_buf.at[slot], slope_hbm.at[i], out_sems.at[slot, 1]),
             )
 
-        ready_tokens(normed, act_buf)
-
-        def image(i, carry):
-            slot = i % 2
-
-            @pl.when(i >= 2)
-            def _():
-                for copy in stores(i - 2, slot):
-                    copy.wait()
-
-            @pl.when(i == 0)
+        for slot in range(4):
+            act_buf[slot, hidden : hidden + 128] = ones_act
+        for n in range(2):
+            normed[n, 192:256] = ones_low
+
+        def pair(g, carry):
+            base = 2 * (g % 2)
+
+            @pl.when(g >= 2)
+            def _():
+                for n in range(2):
+                    for copy in stores(2 * g - 4 + n, base + n):
+                        copy.wait()
+
+            @pl.when(g == 0)
             def _():
                 x_start(0)
                 z_start(2)
 
-            @pl.when(i == 6)
+            @pl.when(g == 4)
             def _():
                 x_start(1)
                 z_start(3)
-                swap_start(0)
-
-            @pl.when(i == 12)
-            def _():
-                x_start(2)
-                z_start(4)
+
+            for n in range(2):
+                unit = take(grad_two_acc, image_rows(2 * g + n))
+                normed[n, 0:patches] = (unit * vectors[0:1] + vectors[1:2]).astype(BF16)
+            pre = [dot(tok_in[...], normed[n]) for n in range(2)]
+            for n in range(2):
+                act, slope = gelu_and_slope(pre[n])
+                act_buf[base + n, 0:hidden] = act.astype(BF16)
+                slope_buf[base + n] = slope.astype(BF16)
+            mixed = [dot(tok_out_t[...], act_buf[base + n]) for n in range(2)]
+            for n in range(2):
+                put(result_acc, image_rows(2 * g + n), mixed[n][0:patches])
+                for copy in stores(2 * g + n, base + n):
+                    copy.start()
+            return carry
+
+        lax.fori_loop(0, images // 2, pair, 0)
+        for i in range(images - 4, images):
+            for copy in stores(i, i % 4):
+                copy.wait()
+        swap_start(0)
+        x_start(2)
+        z_start(4)
+
+        def unit_two_store(b):
+            return pltpu.make_async_copy(unit_buf.at[b % 4], unit_two_hbm.at[span_rows(b)], unit_sems.at[b % 4])
+
+        def span(b, carry):
+            rows = span_rows(b)
+
+            @pl.when(b >= 4)
+            def _():
+                unit_two_store(b - 4).wait()
+
+            mixed = normed_two[rows].astype(F32) + take(result_acc, rows)
+            put(result_acc, rows, mixed)
+            unit, root, _ = row_stats(mixed)
+            stats[rows] = jnp.where(stat_lane < 64, stats[rows], root)
+            unit_buf[b % 4] = unit.astype(BF16)
+            unit_two_store(b).start()
+            normed_two[rows] = (unit * vectors[2:3] + vectors[3:4]).astype(BF16)
+            put(grad_two_acc, rows, jnp.zeros((SPAN, width), F32))
+
+            @pl.when(b == 10)
+            def _():
+                swap_copy(0).wait()
                 swap_start(1)
-
-            unit = take(grad_two_acc, image_rows(i))
-            normed[0:patches] = (unit * vectors[0:1] + vectors[1:2]).astype(BF16)
-            act, slope = gelu_and_slope(dot(tok_in[...], normed[...]))
-            act_buf[slot, 0:hidden] = act.astype(BF16)
-            slope_buf[slot] = slope.astype(BF16)
-            put(result_acc, image_rows(i), dot(tok_out_t[...], act_buf[slot])[0:patches])
-            for copy in stores(i, slot):
-                copy.start()
-            return carry
-
-        lax.fori_loop(0, images, image, 0)
-        for i in (images - 2, images - 1):
-            for copy in stores(i, i % 2):
-                copy.wait()
-        cot_copy.wait()
-
-        def mixed_store(b):
-            return pltpu.make_async_copy(
-                result_acc.at[:, span_rows(b)], mixed_hbm.at[:, span_rows(b)], mixed_sems.at[b]
-            )
-
-        live = jnp.broadcast_to(live_rows(STEP), (STEP, width))
-
-        def span(b, carry):
-            def step(s, inner):
-                rows = span_rows(b, s)
-                mixed = normed_two[rows].astype(F32) + take(result_acc, rows)
-                put(result_acc, rows, mixed)
-                unit, _ = row_stats(mixed)
-                normed_two[rows] = (unit * vectors[2:3] + vectors[3:4]).astype(BF16)
-                grad = grad_rows[rows].astype(F32) * live
-                grad_rows[rows] = grad.astype(BF16)
-                put(grad_two_acc, rows, jnp.zeros((STEP, width), F32))
-                return inner + jnp.sum(grad.reshape(STEP // 8, 8, width), axis=0)
-
-            carry = lax.fori_loop(0, steps, step, carry)
-            mixed_store(b).start()
-
-            @pl.when(b == 4)
-            def _():
                 x_start(3)
                 z_start(5)
 
             return carry
 
-        sums = lax.fori_loop(0, spans, span, jnp.zeros((8, width), F32))
-        vector_sums[4:5] = jnp.sum(sums, axis=0, keepdims=True)
-        for b in range(spans):
-            mixed_store(b).wait()
+        lax.fori_loop(0, spans, span, 0)
+        for b in range(spans - 4, spans):
+            unit_two_store(b).wait()
 
     pl.run_scoped(
         token_forward,
-        pltpu.VMEM((2, hidden + 128, width), BF16),
-        pltpu.VMEM((2, hidden, width), BF16),
-        pltpu.VMEM((256, width), BF16),
-        pltpu.SemaphoreType.DMA((2, 2)),
-        pltpu.SemaphoreType.DMA((spans,)),
+        pltpu.VMEM((4, hidden + 128, width), BF16),
+        pltpu.VMEM((4, hidden, width), BF16),
+        pltpu.VMEM((2, 256, width), BF16),
+        pltpu.VMEM((4, SPAN, width), BF16),
+        pltpu.SemaphoreType.DMA((4, 2)),
+        pltpu.SemaphoreType.DMA((4,)),
     )
 
     def channel(act_all, slope_all, w_in, w_out, load_sems):
@@ -698,7 +709,6 @@
                 for b in range(3)
             ]
 
-        swap_copy(0).wait()
         for copy in loads(0, 0):
             copy.start()
         for copy in loads(0, 0):
@@ -719,7 +729,7 @@
                 grad_act = dot(grad_rows[rows], down, NT)
                 act, slope = gelu_and_slope(pre)
                 grad_pre = grad_act * slope
-                hidden_sums[pl.ds(j, 1)] += jnp.sum(grad_pre, axis=0, keepdims=True)
+                hidden_sums[j] += jnp.sum(grad_pre.reshape(BLOCK // 112, 14, 8, chunk).sum(1), axis=0)
                 act_all[rows] = act.astype(BF16)
                 slope_all[rows] = grad_pre.astype(BF16)
                 forward_part = dot(act_all[rows], down)
@@ -788,22 +798,27 @@
         pltpu.SemaphoreType.DMA((5,)),
     )
 
-    def stage_send(stage, out):
-        return remote(stage, out, end_sems, (0,), partner)
-
-    def stage_own(stage, out):
-        return pltpu.make_async_copy(stage, out, end_sems.at[0, 2])
+    def stage_out_copy(b):
+        return remote(
+            shards.at[:, pl.ds(32 * b, 32)], ch_out_grad.at[:, :, pl.ds(256 * b, 256)], end_sems, (b,), partner
+        )
+
+    def stage_out_own(b):
+        return pltpu.make_async_copy(
+            shards.at[:, pl.ds(32 * b, 32)], ch_out_grad.at[:, :, pl.ds(256 * b, 256)], end_sems.at[0, 4 + b]
+        )
 
     def send_stages():
         @pl.when(c == 0)
         def _():
-            stage_send(stage_in, ch_in_grad).start()
-            stage_own(stage_in, ch_in_grad).start()
+            remote(stage_in, ch_in_grad, end_sems, (0,), partner).start()
+            pltpu.make_async_copy(stage_in, ch_in_grad, end_sems.at[0, 4]).start()
 
         @pl.when(c == 1)
         def _():
-            stage_send(stage_out, ch_out_grad).start()
-            stage_own(stage_out, ch_out_grad).start()
+            for b in range(3):
+                stage_out_copy(b).start()
+                stage_out_own(b).start()
 
     def fill_stages():
         @pl.when(c == 0)
@@ -821,120 +836,141 @@
                     tile = part if tile is None else jnp.where(group == g, part, tile)
                 stage_in[:, LANES * t : LANES * (t + 1)] = tile
 
-        @pl.when(c == 1)
-        def _():
-            for j in range(CHUNKS):
-                for b in range(3):
-                    stage_out[32 * j : 32 * j + 32, 256 * b : 256 * b + 256] = shards[j, 32 * b : 32 * b + 32]
-
-    def token_backward(
-        units, mixed_buf, act_buf, slope_buf, normed, mixed_low, pre_low, out_buf, grad_buf, x_sem, in_sems, mixed_sems, out_sems
-    ):
+    def token_backward(units, unit_buf, out_buf, x_load_sems, in_sems, unit_sems, out_sems):
+        def act_at(slot, count):
+            return normed_two.at[pl.ds(pl.multiple_of(512 * slot, 16), count)]
+
+        def slope_at(slot):
+            return grad_rows.at[pl.ds(pl.multiple_of(384 * slot, 16), hidden)]
+
         def loads(i, slot):
             return (
-                pltpu.make_async_copy(act_hbm.at[i], act_buf.at[slot, pl.ds(0, hidden)], in_sems.at[slot, 0]),
-                pltpu.make_async_copy(slope_hbm.at[i], slope_buf.at[slot], in_sems.at[slot, 1]),
+                pltpu.make_async_copy(act_hbm.at[i], act_at(slot, hidden), in_sems.at[slot, 0]),
+                pltpu.make_async_copy(slope_hbm.at[i], slope_at(slot), in_sems.at[slot, 1]),
             )
 
-        def mixed_load(b, slot):
-            return pltpu.make_async_copy(mixed_hbm.at[:, span_rows(b)], mixed_buf.at[slot], mixed_sems.at[slot])
-
-        x_copy_back = pltpu.make_async_copy(tokens, normed_two, x_sem.at[0])
-        mixed_load(0, 0).start()
-        x_copy_back.start()
+        def unit_two_load(b):
+            return pltpu.make_async_copy(unit_two_hbm.at[span_rows(b)], unit_buf.at[b % 4], unit_sems.at[b % 4])
+
+        def x_load(b):
+            return pltpu.make_async_copy(tokens.at[span_rows(b)], normed_two.at[span_rows(b)], x_load_sems.at[b])
+
         core_copy(1, piece).start()
-        for copy in loads(0, 0):
-            copy.start()
-        ready_tokens(normed, act_buf)
-        mixed_low[192:256] = jnp.zeros((64, width), BF16)
-        x_copy_back.wait()
-
-        def span(b, carry):
+        for b in range(spans):
+            x_load(b).start()
+            if b < 3:
+                unit_two_load(b).start()
+        live = live_rows()
+
+        def out_store(b, slot):
+            return pltpu.make_async_copy(out_buf.at[slot], block_out.at[span_rows(b)], out_sems.at[slot])
+
+        def span(b, sums):
             slot = b % 2
 
-            @pl.when(b + 1 < spans)
-            def _():
-                mixed_load(b + 1, 1 - slot).start()
-
-            mixed_load(b, slot).wait()
-
-            def step(s, sums):
-                rows = span_rows(b, s)
-                inside = pl.ds(pl.multiple_of(s * STEP, 16), STEP)
-                unit, root = row_stats(take(mixed_buf.at[slot], inside))
-                grad = take(grad_two_acc, rows)
-                weighted = grad * unit
-                scaled = grad * vectors[2:3]
-                inner = jnp.mean(scaled * unit, axis=-1, keepdims=True)
-                mixed = grad_rows[rows].astype(F32) + root * (
-                    scaled - jnp.mean(scaled, axis=-1, keepdims=True) - unit * inner
-                )
-                put(grad_two_acc, rows, mixed)
-                unit, _ = row_stats(normed_two[rows].astype(F32))
-                put(units, rows, unit)
-                return (
-                    sums[0] + jnp.sum(weighted.reshape(STEP // 8, 8, width), axis=0),
-                    sums[1] + jnp.sum(grad.reshape(STEP // 8, 8, width), axis=0),
-                )
-
-            carry = lax.fori_loop(0, steps, step, carry)
-
-            @pl.when(b == 6)
+            @pl.when(b + 3 < spans)
+            def _():
+                unit_two_load(b + 3).start()
+
+            @pl.when(b >= 2)
+            def _():
+                out_store(b - 2, slot).wait()
+
+            x_load(b).wait()
+            unit_two_load(b).wait()
+            rows = span_rows(b)
+            put(units, rows, (normed_two[rows].astype(F32) - stats[rows, 32:33]) * stats[rows, 0:1])
+            unit = unit_buf[b % 4].astype(F32)
+            root = stats[rows, 64:65]
+            grad = take(grad_two_acc, rows)
+            weighted = grad * unit
+            scaled = grad * vectors[2:3]
+            inner = jnp.mean(weighted * vectors[2:3], axis=-1, keepdims=True)
+            mixed = grad_rows[rows].astype(F32) + root * (
+                scaled - jnp.mean(scaled, axis=-1, keepdims=True) - unit * inner
+            )
+            put(grad_two_acc, rows, mixed)
+            out_buf[slot] = masked(take(result_acc, rows) + vectors[4:5], live).astype(BF16)
+            out_store(b, slot).start()
+
+            @pl.when(b == 8)
             def _():
                 cross_start(1, piece)
 
-            return carry
+            return sums[0] + row_sum(weighted), sums[1] + row_sum(grad)
 
         zero = jnp.zeros((8, width), F32)
         sums = lax.fori_loop(0, spans, span, (zero, zero))
+        for b in (spans - 2, spans - 1):
+            out_store(b, b % 2).wait()
+        for n in range(2):
+            for copy in loads(n, n):
+                copy.start()
+        for slot in range(4):
+            normed_two[512 * slot + hidden : 512 * slot + 512] = ones_act
+        for n in range(2):
+            normed_two[2048 + 256 * n + 192 : 2048 + 256 * n + 256] = ones_low
+            normed_two[2560 + 256 * n + 192 : 2560 + 256 * n + 256] = jnp.zeros((64, width), BF16)
         vector_sums[2:3] = jnp.sum(sums[0], axis=0, keepdims=True)
         vector_sums[3:4] = jnp.sum(sums[1], axis=0, keepdims=True)
-
-        def image(i, carry):
-            slot = i % 2
-
-            @pl.when(i + 1 < images)
-            def _():
-                for copy in loads(i + 1, 1 - slot):
-                    copy.start()
-
-            for copy in loads(i, slot):
-                copy.wait()
-
-            @pl.when(i == 0)
-            def _():
-                shards[CHUNKS - 2] = line_finish(0, piece)
-
-            @pl.when(i == 5)
+        shards[CHUNKS - 2] = line_finish(0, piece)
+
+        def pair(g, carry):
+            base = 2 * (g % 2)
+
+            @pl.when(g + 1 < images // 2)
+            def _():
+                for n in range(2):
+                    for copy in loads(2 * g + 2 + n, 2 - base + n):
+                        copy.start()
+
+            for n in range(2):
+                for copy in loads(2 * g + n, base + n):
+                    copy.wait()
+
+            @pl.when(g == 3)
             def _():
                 line_start(1, piece)
 
-            @pl.when(i == 11)
+            @pl.when(g == 6)
             def _():
                 shards[CHUNKS - 1] = line_finish(1, piece)
                 fill_stages()
                 send_stages()
 
-            rows = image_rows(i)
-            mixed_low[0:patches] = take(grad_two_acc, rows).astype(BF16)
-            tok_out_sum[...] += dot(act_buf[slot], mixed_low[...], NT)
-            grad_act = dot(tok_out[...], mixed_low[...])
-            pre_low[...] = (grad_act * slope_buf[slot].astype(F32)).astype(BF16)
-            unit = take(units, rows)
-            normed[0:patches] = (unit * vectors[0:1] + vectors[1:2]).astype(BF16)
-            tok_in_sum[...] += dot(pre_low[...], normed[...], NT)
-            grad = dot(tok_in_t[...], pre_low[...])[0:patches]
-            vector_sums[0:1] += jnp.sum(grad * unit, axis=0, keepdims=True)
-            vector_sums[1:2] += jnp.sum(grad, axis=0, keepdims=True)
-            put(units, rows, grad)
+            for n in range(2):
+                low = take(grad_two_acc, image_rows(2 * g + n))
+                normed_two[2560 + 256 * n : 2560 + 256 * n + patches] = low.astype(BF16)
+            unit = [take(units, image_rows(2 * g + n)) for n in range(2)]
+            for n in range(2):
+                normed_two[2048 + 256 * n : 2048 + 256 * n + patches] = (
+                    unit[n] * vectors[0:1] + vectors[1:2]
+                ).astype(BF16)
+            lows = [normed_two[2560 + 256 * n : 2816 + 256 * n] for n in range(2)]
+            grad_act = [dot(tok_out[...], lows[n]) for n in range(2)]
+            for n in range(2):
+                grad_rows[1536 + 384 * n : 1920 + 384 * n] = (
+                    grad_act[n] * slope_at(base + n)[...].astype(F32)
+                ).astype(BF16)
+            tok_out_sum[...] += dot(act_at(base, 512)[...], lows[0], NT) + dot(act_at(base + 1, 512)[...], lows[1], NT)
+            pres = [grad_rows[1536 + 384 * n : 1920 + 384 * n] for n in range(2)]
+            grad = [dot(tok_in_t[...], pres[n])[0:patches] for n in range(2)]
+            tok_in_sum[...] += dot(pres[0], normed_two[2048:2304], NT) + dot(pres[1], normed_two[2304:2560], NT)
+            for n in range(2):
+                put(result_acc, image_rows(2 * g + n), grad[n])
+            gain = grad[0] * unit[0] + grad[1] * unit[1]
+            vector_sums[0:1] += jnp.sum(gain, axis=0, keepdims=True)
+            vector_sums[1:2] += jnp.sum(grad[0] + grad[1], axis=0, keepdims=True)
             return carry
 
-        lax.fori_loop(0, images, image, 0)
+        lax.fori_loop(0, images // 2, pair, 0)
 
         grads[0, :, :, 0:24] = tok_in_sum[...].reshape(4, 4, 24, 256)
         grads[1, :, :, 0:24] = tok_out_sum[0:hidden].reshape(4, 4, 24, 256)
         sums = vector_sums[...]
-        hidden_rows = hidden_sums[...]
+        hidden_rows = jnp.concatenate(
+            [jnp.sum(hidden_sums[j], axis=0, keepdims=True) for j in range(CHUNKS)] + [jnp.zeros((2, 512), F32)], axis=0
+        )
         for o in range(owners):
             moved = sums if o == 0 else pltpu.roll(sums, width - 48 * o, 1)
             grads[0, o // 4, o % 4, 24:32, 0:128] = moved[:, 0:128]
@@ -945,44 +981,32 @@
             grads[1, o // 4, o % 4, 24:32, 128:256] = jnp.zeros((8, 128), F32)
         core_copy(0, 32).start()
 
-        def stores(b, slot):
-            return (
-                pltpu.make_async_copy(out_buf.at[slot], block_out.at[span_rows(b)], out_sems.at[slot, 0]),
-                pltpu.make_async_copy(grad_buf.at[slot], input_grad.at[span_rows(b)], out_sems.at[slot, 1]),
-            )
-
-        live = jnp.broadcast_to(live_rows(STEP), (STEP, width))
+        def grad_store(b, slot):
+            return pltpu.make_async_copy(out_buf.at[slot], input_grad.at[span_rows(b)], out_sems.at[slot])
 
         def last(b, carry):
             slot = b % 2
 
             @pl.when(b >= 2)
             def _():
-                for copy in stores(b - 2, slot):
-                    copy.wait()
-
-            def step(s, inner):
-                rows = span_rows(b, s)
-                inside = pl.ds(pl.multiple_of(s * STEP, 16), STEP)
-                unit, root = row_stats(normed_two[rows].astype(F32))
-                scaled = take(units, rows) * vectors[0:1]
-                mean = jnp.mean(scaled * unit, axis=-1, keepdims=True)
-                grad_buf[slot, inside] = (
-                    take(grad_two_acc, rows)
-                    + root * (scaled - jnp.mean(scaled, axis=-1, keepdims=True) - unit * mean)
-                ).astype(BF16)
-                out_buf[slot, inside] = ((take(result_acc, rows) + vectors[4:5]) * live).astype(BF16)
-                return inner
-
-            lax.fori_loop(0, steps, step, 0)
-            for copy in stores(b, slot):
-                copy.start()
-
-            @pl.when(b == 3)
+                grad_store(b - 2, slot).wait()
+
+            rows = span_rows(b)
+            unit = take(units, rows)
+            root = stats[rows, 0:1]
+            scaled = take(result_acc, rows) * vectors[0:1]
+            inner = jnp.mean(scaled * unit, axis=-1, keepdims=True)
+            out_buf[slot] = (
+                take(grad_two_acc, rows)
+                + root * (scaled - jnp.mean(scaled, axis=-1, keepdims=True) - unit * inner)
+            ).astype(BF16)
+            grad_store(b, slot).start()
+
+            @pl.when(b == 4)
             def _():
                 cross_start(0, 32)
 
-            @pl.when(b == 11)
+            @pl.when(b == spans - 1)
             def _():
                 line_start(0, 32)
 
@@ -990,29 +1014,22 @@
 
         lax.fori_loop(0, spans, last, 0)
         for b in (spans - 2, spans - 1):
-            for copy in stores(b, b % 2):
-                copy.wait()
+            grad_store(b, b % 2).wait()
 
     pl.run_scoped(
         token_backward,
         pltpu.VMEM((tiles, total_rows, LANES), F32),
-        pltpu.VMEM((2, tiles, SPAN, LANES), F32),
-        pltpu.VMEM((2, hidden + 128, width), BF16),
-        pltpu.VMEM((2, hidden, width), BF16),
-        pltpu.VMEM((256, width), BF16),
-        pltpu.VMEM((256, width), BF16),
-        pltpu.VMEM((hidden, width), BF16),
+        pltpu.VMEM((4, SPAN, width), BF16),
         pltpu.VMEM((2, SPAN, width), BF16),
-        pltpu.VMEM((2, SPAN, width), BF16),
-        pltpu.SemaphoreType.DMA((1,)),
-        pltpu.SemaphoreType.DMA((2, 2)),
+        pltpu.SemaphoreType.DMA((spans,)),
+        pltpu.SemaphoreType.DMA((4, 2)),
+        pltpu.SemaphoreType.DMA((4,)),
         pltpu.SemaphoreType.DMA((2,)),
-        pltpu.SemaphoreType.DMA((2, 2)),
     )
 
     small_sum[...] = line_finish(0, 32)
-    small_end = remote(small_sum, small_out.at[c], end_sems, (1,), partner)
-    small_own = pltpu.make_async_copy(small_sum, small_out.at[c], end_sems.at[1, 2])
+    small_end = remote(small_sum, small_out.at[c], end_sems, (3,), partner)
+    small_own = pltpu.make_async_copy(small_sum, small_out.at[c], end_sems.at[1, 4])
     small_end.start()
     small_own.start()
     small_end.wait()
@@ -1020,15 +1037,17 @@
 
     @pl.when(c == 0)
     def _():
-        stage_send(stage_in, ch_in_grad).wait_send()
-        stage_own(stage_in, ch_in_grad).wait()
-        stage_send(stage_out, ch_out_grad).wait_recv()
+        remote(stage_in, ch_in_grad, end_sems, (0,), partner).wait_send()
+        pltpu.make_async_copy(stage_in, ch_in_grad, end_sems.at[0, 4]).wait()
+        for b in range(3):
+            stage_out_copy(b).wait_recv()
 
     @pl.when(c == 1)
     def _():
-        stage_send(stage_out, ch_out_grad).wait_send()
-        stage_own(stage_out, ch_out_grad).wait()
-        stage_send(stage_in, ch_in_grad).wait_recv()
+        for b in range(3):
+            stage_out_copy(b).wait_send()
+            stage_out_own(b).wait()
+        remote(stage_in, ch_in_grad, end_sems, (0,), partner).wait_recv()
 
 
 def finish(small, ch_in_sum, ch_out_sum, *outs):
@@ -1044,8 +1063,14 @@
     tok_out_bias[...] = small[0, 31:32, 0:patches]
     for r, out in enumerate((gain_one, bias_one, gain_two, bias_two, ch_out_bias)):
         out[...] = small[0, 24 + r : 25 + r, 0 : out.shape[1]]
+    each = ch_in_bias.shape[1] // CHUNKS
+    lane = lax.broadcasted_iota(jnp.int32, (1, 256), 1)
+    total = jnp.zeros((1, 256), F32)
     for j in range(CHUNKS):
-        ch_in_bias[j : j + 1] = small[1, 24 + j : 25 + j, 0 : ch_in_bias.shape[1]]
+        part = small[1, 24 + j : 25 + j]
+        part = part if j == 0 else pltpu.roll(part, each * j, 1)
+        total = jnp.where((lane >= each * j) & (lane < each * (j + 1)), part, total)
+    ch_in_bias[...] = total[:, 0 : ch_in_bias.shape[1]]
 
 
 def per_device_fused(
@@ -1065,10 +1090,13 @@
     def by_patch(array):
         return array.transpose(1, 0, 2).reshape(rows, width)
 
-    vector_row = jnp.concatenate(
-        [ln1_gain, ln1_bias, ln2_gain, ln2_bias, ch_out_bias, tok_in_bias, ch_in_bias, tok_out_bias]
-    )
-    vector_row = jnp.pad(vector_row, (0, width - vector_row.shape[0]))[None]
+    vector_row = jnp.zeros((width,), F32)
+    offset = 0
+    for vector in (ln1_gain, ln1_bias, ln2_gain, ln2_bias, ch_out_bias, tok_in_bias, ch_in_bias, tok_out_bias):
+        length = vector.shape[0]
+        vector_row = vector_row + jnp.pad(vector, (offset, width - offset - length)).astype(F32)
+        offset += length
+    vector_row = vector_row[None]
     any_spec = pl.BlockSpec(memory_space=pl.ANY)
     vmem_spec = pl.BlockSpec(memory_space=pltpu.VMEM)
     vmem = pltpu.VMEM
@@ -1083,18 +1111,19 @@
             shape((rows, width), BF16),
             shape((rows, width), BF16),
             shape(ch_in.shape, F32),
-            shape(ch_out.shape, F32),
+            shape((CHUNKS, each, width), F32),
             shape((2, 32, 256), F32),
             shape((2, CHUNKS, 4, 4, 96, 256), BF16),
             shape((images, hidden, width), BF16),
             shape((images, hidden, width), BF16),
-            shape(tiled, F32),
+            shape((rows, width), BF16),
         ],
         scratch_shapes=[
             vmem((rows, width), BF16),
             vmem((rows, width), BF16),
             vmem(tiled, F32),
             vmem(tiled, F32),
+            vmem((rows, LANES), F32),
             vmem((2, 4, 4, 96, 256), F32),
             vmem((2, 4, 4, 96, 256), F32),
             vmem((3, 4, 96, 256), BF16),
@@ -1105,7 +1134,6 @@
             vmem((2, 3, 96, 256), BF16),
             vmem((CHUNKS, 96, 256), F32),
             vmem(ch_in.shape, F32),
-            vmem(ch_out.shape, F32),
             vmem((32, 256), F32),
             vmem((CHUNKS, 96, 256), BF16),
             vmem((2, 4, 4, 32, 256), BF16),
@@ -1116,7 +1144,7 @@
             vmem((8, width), F32),
             vmem((CHUNKS, 1, chunk), F32),
             vmem((8, width), F32),
-            vmem((8, chunk), F32),
+            vmem((CHUNKS, 8, chunk), F32),
             vmem((hidden, 256), F32),
             vmem((hidden + 128, 256), F32),
             dma((2, 7)),
@@ -1127,7 +1155,7 @@
             dma((2, 2)),
             dma((2, 2, 3)),
             dma((2, 2, 3)),
-            dma((2, 3)),
+            dma((2, 7)),
         ],
         compiler_params=pltpu.CompilerParams(
             collective_id=0, has_side_effects=True, vmem_limit_bytes=61 * 1024 * 1024
@@ -1144,10 +1172,10 @@
         out_specs=[vmem_spec] * 12,
         out_shape=[
             line, line, shape(tok_in.shape, F32), shape((1, per_tok), F32), shape(tok_out.shape, F32),
-            shape((1, patches), F32), line, line, shape(ch_in.shape, F32), shape((CHUNKS, each), F32),
+            shape((1, patches), F32), line, line, shape(ch_in.shape, F32), shape((1, per_out), F32),
             shape(ch_out.shape, F32), line,
         ],
-    )(small, in_sum, out_sum)
+    )(small, in_sum, out_sum.reshape(ch_out.shape))
 
     def by_image(array):
         return array.reshape(patches, images, width).transpose(1, 0, 2)

time: 237 us -> 223 us (0.941)
  Pallas kernels: 221 us -> 213 us
  local copies, waits for them, and re-layouts: 14.6 us -> 7.87 us
    pallas_call x1, Pallas kernels: 219 us -> 211 us  [per_device_fused(): pl.pallas_call(mega, in_specs=[pl.BlockSpec(memory_space=pltpu.SMEM), any...]
    concatenate x1 -> x0, local copies, waits for them, and re-layouts: 5.43 us -> none  [per_device_fused(): jnp.concatenate([ln1_gain, ln1_bias, ln2_gain, ln2_bias, ch_out_bias, tok...]
where the time goes in v3:
time: 223 us
  Pallas kernels  213 us (96%)
  local copies, waits for them, and re-layouts  7.87 us (4%)
    pallas_call x1, Pallas kernels, per_device_fused(): pl.pallas_call(mega, in_specs=[pl.BlockSpec(memory_space=pltpu.SMEM), any...  211 us
    unnamed x6, local copies, waits for them, and re-layouts  7.28 us

profile of v3, /device:TPU:0, one launch (start us, length us, event | category | flops | bytes accessed | tf_op | source)
XLA Modules:
  0.0 222.7 jit_solution(3495362551529372023)
XLA Ops:
  0.6 0.9 convert_add_fusion
  1.5 0.6 broadcast_in_dim.3.vector_row
  2.1 210.9 %shard_map.254 = (bf16[3136,768]{1,0:T(8,128)(2,1)}, bf16[3136,768]{1,0:T(8,128)(2,1)}, f32[48,3072]{1,0:T(8,128)}, f32[6,32,768]{2,1,0:T(8,128)}, f32[2,32,256]...) custom-call(s32[1,2]{1,0:T(1,128)} %counts.1, ...), custom_call_target="tpu_custom_call" | custom-call | flops 88785027072 | bytes 100000000 | tf_op jit(solution)/shard_map/pallas_call | solution.py:1106
  213.0 0.0 slice-start
  213.0 2.4 %shard_map.255 = (f32[1,48]{1,0:T(1,128)}, f32[1,48]{1,0:T(1,128)}, f32[24,196]{1,0:T(8,128)}, f32[1,24]{1,0:T(1,128)}, f32[24,196]{1,0:T(8,128)}, /*index=5*/f3...) custom-call(f32[2,32,256]{2,1,0:T(8,128)} %get-tuple-element.33.smal, ...), custom_call_target="tpu_custom_call" | custom-call | tf_op jit(solution)/shard_map/pallas_call | solution.py:1169
  215.4 0.0 slice-start.1
  215.4 5.1 %copy.31 = bf16[16,196,768]{2,0,1:T(8,128)(2,1)} copy(bf16[16,196,768]{2,0,1:T(8,128)(2,1)} %bitcast.24) | data formatting | bytes 9633792
  220.5 0.0 slice-done
  220.5 0.0 slice-done.1
  220.5 2.2 copy.32
  (1 shorter events, 0.0 us)
Async XLA Ops:
  213.0 7.5 %slice-start = ((s8[4816896]{0:T(1024)(128)(4,1)}), s8[622592]{0:T(1024)(128)(4,1)S(1)}, s32[]{:S(2)}) async-start(s8[4816896]{0:T(1024)(128)(4,1)} %bitcast.21), calls=%async_computation | async-start | bytes 1245184
  215.4 5.1 %slice-start.1 = ((s8[4816896]{0:T(1024)(128)(4,1)}), s8[4194304]{0:T(1024)(128)(4,1)S(1)}, s32[]{:S(2)}) async-start(s8[4816896]{0:T(1024)(128)(4,1)} %bitcast.21), calls=%async_computation.1 | async-start | bytes 8388608

commit v4 on v3

--- a/solution.py
+++ b/solution.py
@@ -314,11 +314,11 @@
 def mega(
     counts, tokens, cotangent, vector_row, tok_in_own, tok_out_own, ch_in_own, ch_out_own,
     block_out, input_grad, ch_in_grad, ch_out_grad, small_out, gathered, act_hbm, slope_hbm, unit_two_hbm,
-    normed_two, grad_rows, result_acc, grad_two_acc, stats,
+    normed_two, grad_rows, result_acc, grad_two_acc, stats, w_in, w_out,
     grads, core_in, cross_out, cross_keep, cross_in, line_out, line_keep, line_in, shards, stage_in,
     small_sum, own_weights, small, tok_in, tok_in_t, tok_out, tok_out_t, vectors, hidden_bias,
     vector_sums, hidden_sums, tok_in_sum, tok_out_sum,
-    small_sems, z_sems, z_local, x_sems, swap_sems, core_sems, cross_sems, line_sems, end_sems,
+    small_sems, z_sems, z_local, x_sems, swap_sems, core_sems, cross_sems, line_sems, end_sems, load_sems, weight_sems,
 ):
     total_rows, width = tokens.shape
     images, hidden = act_hbm.shape[0], act_hbm.shape[1]
@@ -343,6 +343,20 @@
             device_id=device, device_id_type=MESH,
         )
 
+    def span_rows(b):
+        return pl.ds(pl.multiple_of(b * SPAN, 16), SPAN)
+
+    spans = total_rows // SPAN
+
+    def row_loads(b):
+        return (
+            pltpu.make_async_copy(tokens.at[span_rows(b)], normed_two.at[span_rows(b)], load_sems.at[0, b]),
+            pltpu.make_async_copy(cotangent.at[span_rows(b)], grad_rows.at[span_rows(b)], load_sems.at[1, b]),
+        )
+
+    for b in range(spans):
+        for copy in row_loads(b):
+            copy.start()
     barrier = pltpu.get_barrier_semaphore()
     for device in [partner] + [cross(k) for k in (1, 2, 3)] + [line(k) for k in (1, 2, 3)]:
         pl.semaphore_signal(barrier, inc=1, device_id=device, device_id_type=MESH)
@@ -477,11 +491,6 @@
         return jnp.sum(value.reshape(4, SPAN // 32, 8, width).sum(1), axis=0)
 
     stat_lane = lax.broadcasted_iota(jnp.int32, (SPAN, LANES), 1)
-
-    def span_rows(b):
-        return pl.ds(pl.multiple_of(b * SPAN, 16), SPAN)
-
-    spans = total_rows // SPAN
 
     def image_rows(i):
         return pl.ds(i, patches, stride=images)
@@ -508,16 +517,7 @@
                 for b in range(3):
                     own_weights[j, 32 * b : 32 * b + 32] = ch_out_own[32 * j : 32 * j + 32, 256 * b : 256 * b + 256]
 
-    def norm_one(load_sems):
-        def loads(b):
-            return (
-                pltpu.make_async_copy(tokens.at[span_rows(b)], normed_two.at[span_rows(b)], load_sems.at[0, b]),
-                pltpu.make_async_copy(cotangent.at[span_rows(b)], grad_rows.at[span_rows(b)], load_sems.at[1, b]),
-            )
-
-        for b in range(spans):
-            for copy in loads(b):
-                copy.start()
+    def norm_one():
         pl.semaphore_wait(barrier, 7)
         for k in (1, 2, 3):
             small_line(k).start()
@@ -526,7 +526,7 @@
         live = live_rows()
 
         def span(b, carry):
-            for copy in loads(b):
+            for copy in row_loads(b):
                 copy.wait()
             rows = span_rows(b)
             unit, root, mean = row_stats(normed_two[rows].astype(F32))
@@ -554,10 +554,7 @@
         sums = lax.fori_loop(0, spans, span, jnp.zeros((8, width), F32))
         vector_sums[...] = jnp.zeros(vector_sums.shape, F32)
         vector_sums[4:5] = jnp.sum(sums, axis=0, keepdims=True)
-    pl.run_scoped(
-        norm_one,
-        pltpu.SemaphoreType.DMA((2, spans)),
-    )
+    norm_one()
     hidden_sums[...] = jnp.zeros(hidden_sums.shape, F32)
     tok_in_sum[...] = jnp.zeros(tok_in_sum.shape, F32)
     tok_out_sum[...] = jnp.zeros(tok_out_sum.shape, F32)
@@ -593,6 +590,20 @@
         rows = dot(pick, jnp.where(own_n == own_p, dot(flat_a, spread), 0.0).astype(BF16))
         hidden_bias[j] = rows[5:6]
 
+    def weight_loads(j, p):
+        return [
+            pltpu.make_async_copy(
+                gathered.at[0, j, :, :, pl.ds(48 * b, 48)], w_in.at[p, :, :, :, pl.ds(256 * b, 256)], weight_sems.at[b]
+            )
+            for b in range(2)
+        ] + [
+            pltpu.make_async_copy(
+                gathered.at[1, j, :, :, pl.ds(32 * b, 32)], w_out.at[p, :, :, :, pl.ds(256 * b, 256)],
+                weight_sems.at[2 + b],
+            )
+            for b in range(3)
+        ]
+
     ones_low = jnp.where(lax.broadcasted_iota(jnp.int32, (64, width), 0) == 8, 1.0, 0.0).astype(BF16)
     ones_act = jnp.where(lax.broadcasted_iota(jnp.int32, (128, width), 0) == 0, 1.0, 0.0).astype(BF16)
 
@@ -608,9 +619,7 @@
         for n in range(2):
             normed[n, 192:256] = ones_low
 
-        def pair(g, carry):
-            base = 2 * (g % 2)
-
+        def pair(g, base):
             @pl.when(g >= 2)
             def _():
                 for n in range(2):
@@ -640,9 +649,13 @@
                 put(result_acc, image_rows(2 * g + n), mixed[n][0:patches])
                 for copy in stores(2 * g + n, base + n):
                     copy.start()
+
+        def pairs(h, carry):
+            for half in range(2):
+                pair(2 * h + half, 2 * half)
             return carry
 
-        lax.fori_loop(0, images // 2, pair, 0)
+        lax.fori_loop(0, images // 4, pairs, 0)
         for i in range(images - 4, images):
             for copy in stores(i, i % 4):
                 copy.wait()
@@ -672,6 +685,8 @@
             @pl.when(b == 10)
             def _():
                 swap_copy(0).wait()
+                for copy in weight_loads(0, 0):
+                    copy.start()
                 swap_start(1)
                 x_start(3)
                 z_start(5)
@@ -692,26 +707,10 @@
         pltpu.SemaphoreType.DMA((4,)),
     )
 
-    def channel(act_all, slope_all, w_in, w_out, load_sems):
+    def channel(act_all, slope_all):
         chunk = w_in.shape[-1]
 
-        def loads(j, p):
-            return [
-                pltpu.make_async_copy(
-                    gathered.at[0, j, :, :, pl.ds(48 * b, 48)], w_in.at[p, :, :, :, pl.ds(256 * b, 256)], load_sems.at[b]
-                )
-                for b in range(2)
-            ] + [
-                pltpu.make_async_copy(
-                    gathered.at[1, j, :, :, pl.ds(32 * b, 32)], w_out.at[p, :, :, :, pl.ds(256 * b, 256)],
-                    load_sems.at[2 + b],
-                )
-                for b in range(3)
-            ]
-
-        for copy in loads(0, 0):
-            copy.start()
-        for copy in loads(0, 0):
+        for copy in weight_loads(0, 0):
             copy.wait()
 
         def tick(j, carry):
@@ -739,7 +738,11 @@
                 for t in range(tiles):
                     grad_two_acc[t, rows] += backward_part[:, LANES * t : LANES * (t + 1)]
 
-                @pl.when((b == 0) & (j >= 1))
+                @pl.when((b == 0) & (j >= 2))
+                def _():
+                    line_start(p, piece)
+
+                @pl.when((b == 1) & (j >= 1))
                 def _():
                     cross_start(1 - p, piece)
 
@@ -756,10 +759,10 @@
                 def _():
                     shards[j - 2] = line_finish(p, piece)
 
-                @pl.when((b == 1) & (j + 1 < CHUNKS))
+                @pl.when((b == 2) & (j + 1 < CHUNKS))
                 def _():
                     swap_copy(j + 1).wait()
-                    for copy in loads(j + 1, 1 - p):
+                    for copy in weight_loads(j + 1, 1 - p):
                         copy.start()
 
                 @pl.when((b == 3) & (j + 3 < CHUNKS))
@@ -776,13 +779,9 @@
             for b in range(3):
                 grads[1, :, :, 32 * b : 32 * b + 32] = down_grad[:, 256 * b : 256 * b + 256].reshape(4, 4, 32, 256)
 
-            @pl.when(j >= 1)
-            def _():
-                line_start(1 - p, piece)
-
             @pl.when(j + 1 < CHUNKS)
             def _():
-                for copy in loads(j + 1, 1 - p):
+                for copy in weight_loads(j + 1, 1 - p):
                     copy.wait()
 
             return carry
@@ -793,9 +792,6 @@
         channel,
         pltpu.VMEM((total_rows, 512), BF16),
         pltpu.VMEM((total_rows, 512), BF16),
-        pltpu.VMEM((2, 4, 4, 48, 512), BF16),
-        pltpu.VMEM((2, 4, 4, 32, 768), BF16),
-        pltpu.SemaphoreType.DMA((5,)),
     )
 
     def stage_out_copy(b):
@@ -838,10 +834,10 @@
 
     def token_backward(units, unit_buf, out_buf, x_load_sems, in_sems, unit_sems, out_sems):
         def act_at(slot, count):
-            return normed_two.at[pl.ds(pl.multiple_of(512 * slot, 16), count)]
+            return normed_two.at[pl.ds(512 * slot, count)]
 
         def slope_at(slot):
-            return grad_rows.at[pl.ds(pl.multiple_of(384 * slot, 16), hidden)]
+            return grad_rows.at[pl.ds(384 * slot, hidden)]
 
         def loads(i, slot):
             return (
@@ -893,7 +889,11 @@
             out_buf[slot] = masked(take(result_acc, rows) + vectors[4:5], live).astype(BF16)
             out_store(b, slot).start()
 
-            @pl.when(b == 8)
+            @pl.when(b == 2)
+            def _():
+                line_start(0, piece)
+
+            @pl.when(b == 7)
             def _():
                 cross_start(1, piece)
 
@@ -915,9 +915,7 @@
         vector_sums[3:4] = jnp.sum(sums[1], axis=0, keepdims=True)
         shards[CHUNKS - 2] = line_finish(0, piece)
 
-        def pair(g, carry):
-            base = 2 * (g % 2)
-
+        def pair(g, base):
             @pl.when(g + 1 < images // 2)
             def _():
                 for n in range(2):
@@ -961,9 +959,13 @@
             gain = grad[0] * unit[0] + grad[1] * unit[1]
             vector_sums[0:1] += jnp.sum(gain, axis=0, keepdims=True)
             vector_sums[1:2] += jnp.sum(grad[0] + grad[1], axis=0, keepdims=True)
+
+        def pairs(h, carry):
+            for half in range(2):
+                pair(2 * h + half, 2 * half)
             return carry
 
-        lax.fori_loop(0, images // 2, pair, 0)
+        lax.fori_loop(0, images // 4, pairs, 0)
 
         grads[0, :, :, 0:24] = tok_in_sum[...].reshape(4, 4, 24, 256)
         grads[1, :, :, 0:24] = tok_out_sum[0:hidden].reshape(4, 4, 24, 256)
@@ -1124,6 +1126,8 @@
             vmem(tiled, F32),
             vmem(tiled, F32),
             vmem((rows, LANES), F32),
+            vmem((2, 4, 4, per_in, chunk), BF16),
+            vmem((2, 4, 4, each, width), BF16),
             vmem((2, 4, 4, 96, 256), F32),
             vmem((2, 4, 4, 96, 256), F32),
             vmem((3, 4, 96, 256), BF16),
@@ -1156,6 +1160,8 @@
             dma((2, 2, 3)),
             dma((2, 2, 3)),
             dma((2, 7)),
+            dma((2, 14)),
+            dma((5,)),
         ],
         compiler_params=pltpu.CompilerParams(
             collective_id=0, has_side_effects=True, vmem_limit_bytes=61 * 1024 * 1024

time: 223 us -> 219 us (0.982)
  Pallas kernels: 213 us -> 210 us
    pallas_call x1, Pallas kernels: 211 us -> 207 us  [per_device_fused(): pl.pallas_call(mega, in_specs=[pl.BlockSpec(memory_space=pltpu.SMEM), any...]
where the time goes in v4:
time: 219 us
  Pallas kernels  210 us (96%)
  local copies, waits for them, and re-layouts  7.87 us (4%)
    pallas_call x1, Pallas kernels, per_device_fused(): pl.pallas_call(mega, in_specs=[pl.BlockSpec(memory_space=pltpu.SMEM), any...  207 us
    unnamed x6, local copies, waits for them, and re-layouts  7.28 us

profile of v4, /device:TPU:0, one launch (start us, length us, event | category | flops | bytes accessed | tf_op | source)
XLA Modules:
  0.0 219.0 jit_solution(4473275084009725524)
XLA Ops:
  0.6 0.9 convert_add_fusion
  1.5 0.6 broadcast_in_dim.3.vector_row
  2.1 207.2 %shard_map.254 = (bf16[3136,768]{1,0:T(8,128)(2,1)}, bf16[3136,768]{1,0:T(8,128)(2,1)}, f32[48,3072]{1,0:T(8,128)}, f32[6,32,768]{2,1,0:T(8,128)}, f32[2,32,256]...) custom-call(s32[1,2]{1,0:T(1,128)} %counts.1, ...), custom_call_target="tpu_custom_call" | custom-call | flops 88785027072 | bytes 100000000 | tf_op jit(solution)/shard_map/pallas_call | solution.py:1108
  209.3 0.0 slice-start
  209.3 2.4 %shard_map.255 = (f32[1,48]{1,0:T(1,128)}, f32[1,48]{1,0:T(1,128)}, f32[24,196]{1,0:T(8,128)}, f32[1,24]{1,0:T(1,128)}, f32[24,196]{1,0:T(8,128)}, /*index=5*/f3...) custom-call(f32[2,32,256]{2,1,0:T(8,128)} %get-tuple-element.33.smal, ...), custom_call_target="tpu_custom_call" | custom-call | tf_op jit(solution)/shard_map/pallas_call | solution.py:1175
  211.7 0.0 slice-start.1
  211.7 5.1 %copy.31 = bf16[16,196,768]{2,0,1:T(8,128)(2,1)} copy(bf16[16,196,768]{2,0,1:T(8,128)(2,1)} %bitcast.24) | data formatting | bytes 9633792
  216.8 0.0 slice-done
  216.8 0.0 slice-done.1
  216.8 2.2 %copy.32 = bf16[16,196,768]{2,0,1:T(8,128)(2,1)} copy(bf16[16,196,768]{2,0,1:T(8,128)(2,1)S(1)} %bitcast.23) | data formatting | bytes 9633792
  (1 shorter events, 0.0 us)
Async XLA Ops:
  209.3 7.5 %slice-start = ((s8[4816896]{0:T(1024)(128)(4,1)}), s8[622592]{0:T(1024)(128)(4,1)S(1)}, s32[]{:S(2)}) async-start(s8[4816896]{0:T(1024)(128)(4,1)} %bitcast.21), calls=%async_computation | async-start | bytes 1245184
  211.7 5.1 %slice-start.1 = ((s8[4816896]{0:T(1024)(128)(4,1)}), s8[4194304]{0:T(1024)(128)(4,1)S(1)}, s32[]{:S(2)}) async-start(s8[4816896]{0:T(1024)(128)(4,1)} %bitcast.21), calls=%async_computation.1 | async-start | bytes 8388608

commit v5 on v4

--- a/solution.py
+++ b/solution.py
@@ -277,6 +277,7 @@
 BLOCK = 784
 SPAN = 224
 LANES = 128
+ROOM = 200
 C_A = 0.7978845608
 C_B = 0.7978845608 * 0.044715
 
@@ -348,15 +349,25 @@
 
     spans = total_rows // SPAN
 
-    def row_loads(b):
+    parts = total_rows // (16 * images)
+    rest = total_rows - parts * 16 * images
+
+    def part_rows(b):
+        return pl.ds(pl.multiple_of(b * 16 * images, 16), 16 * images)
+
+    last_part = pl.ds(parts * 16 * images, rest)
+
+    def row_loads(b, rows):
         return (
-            pltpu.make_async_copy(tokens.at[span_rows(b)], normed_two.at[span_rows(b)], load_sems.at[0, b]),
-            pltpu.make_async_copy(cotangent.at[span_rows(b)], grad_rows.at[span_rows(b)], load_sems.at[1, b]),
-        )
-
-    for b in range(spans):
-        for copy in row_loads(b):
+            pltpu.make_async_copy(tokens.at[rows], normed_two.at[rows], load_sems.at[0, b]),
+            pltpu.make_async_copy(cotangent.at[rows], grad_rows.at[rows], load_sems.at[1, b]),
+        )
+
+    for b in range(parts):
+        for copy in row_loads(b, part_rows(b)):
             copy.start()
+    for copy in row_loads(parts, last_part):
+        copy.start()
     barrier = pltpu.get_barrier_semaphore()
     for device in [partner] + [cross(k) for k in (1, 2, 3)] + [line(k) for k in (1, 2, 3)]:
         pl.semaphore_signal(barrier, inc=1, device_id=device, device_id_type=MESH)
@@ -485,10 +496,10 @@
         return jnp.broadcast_to(live, (images, width))
 
     def masked(value, live):
-        return (value.reshape(SPAN // images, images, width) * live[None]).reshape(SPAN, width)
+        return (value.reshape(-1, images, width) * live[None]).reshape(value.shape)
 
     def row_sum(value):
-        return jnp.sum(value.reshape(4, SPAN // 32, 8, width).sum(1), axis=0)
+        return jnp.sum(value.reshape(4, value.shape[0] // 32, 8, width).sum(1), axis=0)
 
     stat_lane = lax.broadcasted_iota(jnp.int32, (SPAN, LANES), 1)
 
@@ -525,15 +536,24 @@
         z_start(0)
         live = live_rows()
 
-        def span(b, carry):
-            for copy in row_loads(b):
+        def part(b, rows):
+            count = rows.size
+            each = count // images
+            for copy in row_loads(b, rows):
                 copy.wait()
-            rows = span_rows(b)
             unit, root, mean = row_stats(normed_two[rows].astype(F32))
-            put(grad_two_acc, rows, unit)
-            stats[rows] = jnp.where(stat_lane < 32, root, mean)
+            for t in range(tiles):
+                by_image = jnp.swapaxes(unit[:, LANES * t : LANES * (t + 1)].reshape(each, images, LANES), 0, 1)
+                for i in range(images):
+                    grad_two_acc[t, pl.ds(pl.multiple_of(ROOM * i + 16 * b, 8), each)] = by_image[i]
+            stat = lax.broadcasted_iota(jnp.int32, (count, LANES), 1)
+            stats[rows] = jnp.where(stat < 32, root, mean)
             grad = masked(grad_rows[rows].astype(F32), live)
             grad_rows[rows] = grad.astype(BF16)
+            return row_sum(grad)
+
+        def step(b, carry):
+            carry = carry + part(b, part_rows(b))
 
             @pl.when(b == 4)
             def _():
@@ -543,15 +563,16 @@
                     small_cross(k).start()
                 z_start(1)
 
-            @pl.when(b == 10)
+            @pl.when(b == 9)
             def _():
                 for k in (1, 2, 3):
                     small_cross(k).wait()
                 small_swap().start()
 
-            return carry + row_sum(grad)
-
-        sums = lax.fori_loop(0, spans, span, jnp.zeros((8, width), F32))
+            return carry
+
+        sums = lax.fori_loop(0, parts, step, jnp.zeros((8, width), F32))
+        sums = sums + part(parts, last_part)
         vector_sums[...] = jnp.zeros(vector_sums.shape, F32)
         vector_sums[4:5] = jnp.sum(sums, axis=0, keepdims=True)
     norm_one()
@@ -637,7 +658,7 @@
                 z_start(3)
 
             for n in range(2):
-                unit = take(grad_two_acc, image_rows(2 * g + n))
+                unit = take(grad_two_acc, pl.ds(pl.multiple_of(ROOM * (2 * g + n), 8), patches))
                 normed[n, 0:patches] = (unit * vectors[0:1] + vectors[1:2]).astype(BF16)
             pre = [dot(tok_in[...], normed[n]) for n in range(2)]
             for n in range(2):
@@ -1124,7 +1145,7 @@
             vmem((rows, width), BF16),
             vmem((rows, width), BF16),
             vmem(tiled, F32),
-            vmem(tiled, F32),
+            vmem((width // LANES, images * ROOM, LANES), F32),
             vmem((rows, LANES), F32),
             vmem((2, 4, 4, per_in, chunk), BF16),
             vmem((2, 4, 4, each, width), BF16),

time: 219 us -> 216 us (0.986)
  Pallas kernels: 210 us -> 207 us
    pallas_call x1, Pallas kernels: 207 us -> 204 us  [per_device_fused(): pl.pallas_call(mega, in_specs=[pl.BlockSpec(memory_space=pltpu.SMEM), any...]
where the time goes in v5:
time: 216 us
  Pallas kernels  207 us (96%)
  local copies, waits for them, and re-layouts  7.87 us (4%)
    pallas_call x1, Pallas kernels, per_device_fused(): pl.pallas_call(mega, in_specs=[pl.BlockSpec(memory_space=pltpu.SMEM), any...  204 us
    unnamed x6, local copies, waits for them, and re-layouts  7.28 us

profile of v5, /device:TPU:0, one launch (start us, length us, event | category | flops | bytes accessed | tf_op | source)
XLA Modules:
  0.0 215.9 jit_solution(1335261425608388445)
XLA Ops:
  0.6 0.9 convert_add_fusion
  1.5 0.6 broadcast_in_dim.3.vector_row
  2.1 204.1 %shard_map.254 = (bf16[3136,768]{1,0:T(8,128)(2,1)}, bf16[3136,768]{1,0:T(8,128)(2,1)}, f32[48,3072]{1,0:T(8,128)}, f32[6,32,768]{2,1,0:T(8,128)}, f32[2,32,256]...) custom-call(s32[1,2]{1,0:T(1,128)} %counts.1, ...), custom_call_target="tpu_custom_call" | custom-call | flops 88785027072 | bytes 100000000 | tf_op jit(solution)/shard_map/pallas_call | solution.py:1129
  206.2 0.0 slice-start
  206.2 2.4 %shard_map.255 = (f32[1,48]{1,0:T(1,128)}, f32[1,48]{1,0:T(1,128)}, f32[24,196]{1,0:T(8,128)}, f32[1,24]{1,0:T(1,128)}, f32[24,196]{1,0:T(8,128)}, /*index=5*/f3...) custom-call(f32[2,32,256]{2,1,0:T(8,128)} %get-tuple-element.33.smal, ...), custom_call_target="tpu_custom_call" | custom-call | tf_op jit(solution)/shard_map/pallas_call | solution.py:1196
  208.6 0.0 slice-start.1
  208.7 5.1 %copy.31 = bf16[16,196,768]{2,0,1:T(8,128)(2,1)} copy(bf16[16,196,768]{2,0,1:T(8,128)(2,1)} %bitcast.24) | data formatting | bytes 9633792
  213.7 0.0 slice-done
  213.7 0.0 slice-done.1
  213.7 2.2 %copy.32 = bf16[16,196,768]{2,0,1:T(8,128)(2,1)} copy(bf16[16,196,768]{2,0,1:T(8,128)(2,1)S(1)} %bitcast.23) | data formatting | bytes 9633792
  (1 shorter events, 0.0 us)
Async XLA Ops:
  206.2 7.5 %slice-start = ((s8[4816896]{0:T(1024)(128)(4,1)}), s8[622592]{0:T(1024)(128)(4,1)S(1)}, s32[]{:S(2)}) async-start(s8[4816896]{0:T(1024)(128)(4,1)} %bitcast.21), calls=%async_computation | async-start | bytes 1245184
  208.6 5.1 %slice-start.1 = ((s8[4816896]{0:T(1024)(128)(4,1)}), s8[4194304]{0:T(1024)(128)(4,1)S(1)}, s32[]{:S(2)}) async-start(s8[4816896]{0:T(1024)(128)(4,1)} %bitcast.21), calls=%async_computation.1 | async-start | bytes 8388608

commit v6 on v5

--- a/solution.py
+++ b/solution.py
@@ -555,7 +555,7 @@
         def step(b, carry):
             carry = carry + part(b, part_rows(b))
 
-            @pl.when(b == 4)
+            @pl.when(b == 3)
             def _():
                 for k in (1, 2, 3):
                     small_line(k).wait()
@@ -1025,11 +1025,11 @@
             ).astype(BF16)
             grad_store(b, slot).start()
 
-            @pl.when(b == 4)
+            @pl.when(b == 3)
             def _():
                 cross_start(0, 32)
 
-            @pl.when(b == spans - 1)
+            @pl.when(b == spans - 3)
             def _():
                 line_start(0, 32)
 

time: 216 us -> 216 us (level)
  no operation moved by 1% of the time
where the time goes in v6:
time: 216 us
  Pallas kernels  207 us (96%)
  local copies, waits for them, and re-layouts  7.87 us (4%)
    pallas_call x1, Pallas kernels, per_device_fused(): pl.pallas_call(mega, in_specs=[pl.BlockSpec(memory_space=pltpu.SMEM), any...  204 us
    unnamed x6, local copies, waits for them, and re-layouts  7.28 us

profile of v6, /device:TPU:0, one launch (start us, length us, event | category | flops | bytes accessed | tf_op | source)
XLA Modules:
  0.0 215.9 jit_solution(9472632960346351368)
XLA Ops:
  0.6 0.9 convert_add_fusion
  1.5 0.6 broadcast_in_dim.3.vector_row
  2.1 204.1 %shard_map.254 = (bf16[3136,768]{1,0:T(8,128)(2,1)}, bf16[3136,768]{1,0:T(8,128)(2,1)}, f32[48,3072]{1,0:T(8,128)}, f32[6,32,768]{2,1,0:T(8,128)}, f32[2,32,256]...) custom-call(s32[1,2]{1,0:T(1,128)} %counts.1, ...), custom_call_target="tpu_custom_call" | custom-call | flops 88785027072 | bytes 100000000 | tf_op jit(solution)/shard_map/pallas_call | solution.py:1129
  206.2 0.0 slice-start
  206.2 2.4 %shard_map.255 = (f32[1,48]{1,0:T(1,128)}, f32[1,48]{1,0:T(1,128)}, f32[24,196]{1,0:T(8,128)}, f32[1,24]{1,0:T(1,128)}, f32[24,196]{1,0:T(8,128)}, /*index=5*/f3...) custom-call(f32[2,32,256]{2,1,0:T(8,128)} %get-tuple-element.33.smal, ...), custom_call_target="tpu_custom_call" | custom-call | tf_op jit(solution)/shard_map/pallas_call | solution.py:1196
  208.6 0.0 slice-start.1
  208.7 5.1 %copy.31 = bf16[16,196,768]{2,0,1:T(8,128)(2,1)} copy(bf16[16,196,768]{2,0,1:T(8,128)(2,1)} %bitcast.24) | data formatting | bytes 9633792
  213.7 0.0 slice-done
  213.7 0.0 slice-done.1
  213.7 2.2 %copy.32 = bf16[16,196,768]{2,0,1:T(8,128)(2,1)} copy(bf16[16,196,768]{2,0,1:T(8,128)(2,1)S(1)} %bitcast.23) | data formatting | bytes 9633792
  (1 shorter events, 0.0 us)
Async XLA Ops:
  206.2 7.5 %slice-start = ((s8[4816896]{0:T(1024)(128)(4,1)}), s8[622592]{0:T(1024)(128)(4,1)S(1)}, s32[]{:S(2)}) async-start(s8[4816896]{0:T(1024)(128)(4,1)} %bitcast.21), calls=%async_computation | async-start | bytes 1245184
  208.6 5.1 %slice-start.1 = ((s8[4816896]{0:T(1024)(128)(4,1)}), s8[4194304]{0:T(1024)(128)(4,1)S(1)}, s32[]{:S(2)}) async-start(s8[4816896]{0:T(1024)(128)(4,1)} %bitcast.21), calls=%async_computation.1 | async-start | bytes 8388608
